TPU v7x, 128 devices: a whole 4x4x4 slice. The times are simulated.
128 devices in a mesh: tt: 8 (over z_lo, x), sv: 16 (over z_hi, y, core).
Axes of the slice: x: 4, y: 4, z: 4 (z_hi: 2, z_lo: 2; z = z_hi * 2 + z_lo), core: 2. Of those that a mesh axis runs over, the one named last changes fastest.
Arguments:
- teacher_hidden: bfloat16 [256, 16384], P(None, 'sv'), may hold values from -620 to 620
- teacher_head: bfloat16 [16384, 65536], P('sv', 'tt'), may hold values from -0.046875 to 0.046875
- student_hidden: bfloat16 [256, 4096], P(('tt', 'sv')), may hold values from -42 to 42
- student_head: bfloat16 [4096, 65536], P(None, ('tt', 'sv')), may hold values from -1.5 to 1.5
- targets: int32 [256], replicated, may hold values from 0 to 65535
Outputs:
- loss: float32 [], replicated
- head_grad: bfloat16 [4096, 65536], P(None, ('tt', 'sv'))
- hidden_grad: float32 [256, 4096], P(('tt', 'sv'))
All inputs are finite; a program needn't handle non-finite values.
Results may differ from a plain program's by a relative error of at most 0.0038.
Values may be sent and summed in bfloat16 or wider, within the bound.
No kernel may reach another device: no remote copies, remote signals or barrier semaphores. Data moves between devices by JAX's collectives and lax.ppermute only.
A program may use at most 128 MiB of HBM per device.

v0:
```python
import jax
import jax.numpy as jnp
from jax import lax
from jax.sharding import PartitionSpec as P

ce_weight = 0.5


def merged(value, axis, join):
    pieces = jax.tree.map(lambda part: lax.all_gather(part, axis), value)
    head = jax.tree.map(lambda part: part[0], pieces)
    tail = jax.tree.map(lambda part: part[1:], pieces)
    total, _ = lax.scan(lambda total, piece: (join(total, piece), None), head, tail)
    return total


def combine_pair(first, second):
    top = jnp.maximum(first[0], second[0])
    total = first[1] * jnp.exp(first[0] - top) + second[1] * jnp.exp(second[0] - top)
    return (top, total)


def combine_stats(first, second):
    top, total = combine_pair(first[:2], second[:2])
    return (
        top,
        total,
        first[2] + second[2],
        first[3] + second[3],
        first[4] + second[4],
        first[5] + second[5],
    )


def body(teacher_hidden, teacher_head, student_hidden, student_head, targets):
    tokens = teacher_hidden.shape[0]
    vocab_dev = student_head.shape[1]
    rows = teacher_hidden
    logits_t = lax.psum_scatter(
        jnp.dot(rows, teacher_head, preferred_element_type=jnp.float32),
        "sv",
        scatter_dimension=0,
        tiled=True,
    )
    top_t = jnp.max(logits_t, axis=1)
    total_t = jnp.sum(jnp.exp(logits_t - top_t[:, None]), axis=1)
    top_t, total_t = merged((top_t, total_t), "tt", combine_pair)
    log_t = logits_t - (top_t + jnp.log(total_t))[:, None]
    rounded = lax.optimization_barrier(jnp.exp(log_t).astype(jnp.bfloat16))
    entropy = jnp.sum(rounded.astype(jnp.float32) * log_t)
    probs = lax.all_to_all(rounded, "sv", split_axis=1, concat_axis=0, tiled=True)
    hidden_all = lax.all_gather(student_hidden, ("tt", "sv"), axis=0, tiled=True)
    logits_s = jnp.dot(hidden_all, student_head, preferred_element_type=jnp.float32)
    offset = lax.axis_index(("tt", "sv")) * vocab_dev
    columns = offset + lax.broadcasted_iota(jnp.int32, (1, vocab_dev), 1)
    hit = (columns == targets[:, None]).astype(jnp.float32)
    probs_f = probs.astype(jnp.float32)
    top_s = jnp.max(logits_s, axis=1)
    total_s = jnp.sum(jnp.exp(logits_s - top_s[:, None]), axis=1)
    cross = jnp.sum(probs_f * logits_s, axis=1)
    mass = jnp.sum(probs_f, axis=1)
    picked = jnp.sum(hit * logits_s, axis=1)
    top_s, total_s, cross, mass, picked, entropy = merged(
        (top_s, total_s, cross, mass, picked, entropy), ("tt", "sv"), combine_stats
    )
    norm_s = top_s + jnp.log(total_s)
    loss = (
        entropy - jnp.sum(cross - mass * norm_s) + ce_weight * jnp.sum(norm_s - picked)
    ) / tokens
    probs_s = jnp.exp(logits_s - norm_s[:, None])
    grad_logits = ((mass + ce_weight)[:, None] * probs_s - probs_f - ce_weight * hit).astype(
        jnp.bfloat16
    )
    head_grad = lax.dot_general(
        hidden_all, grad_logits, (((0,), (0,)), ((), ())), preferred_element_type=jnp.float32
    ).astype(jnp.bfloat16)
    rows = grad_logits
    hidden_grad = lax.psum_scatter(
        lax.dot_general(
            rows, student_head, (((1,), (1,)), ((), ())), preferred_element_type=jnp.float32
        ),
        ("tt", "sv"),
        scatter_dimension=0,
        tiled=True,
    )
    return (loss, head_grad, hidden_grad)


def solution(mesh):
    placed = (P(None, "sv"), P("sv", "tt"), P(("tt", "sv"), None), P(None, ("tt", "sv")), P())
    return jax.shard_map(
        body,
        mesh=mesh,
        in_specs=placed,
        out_specs=(P(), P(None, ("tt", "sv")), P(("tt", "sv"), None)),
        check_vma=False,
    )
```

profile of v0, /device:TPU:0, one launch (start us, length us, event | category | flops | bytes accessed | tf_op | source)
XLA Modules:
  0.0 1919.6 jit_solution(8462369748419158129)
XLA Ops:
  9.0 12.5 fusion.12
  23.4 205.2 %all-gather.14.cloned.1.call-done = bf16[128,2,4096]{2,1,0:T(2,128)(2,1)} async-done(((bf16[1,2,4096]{2,1,0:T(2,128)(2,1)}), bf16[128,2,4096]{2,1,0:T(2,128)(2,1)}) %all-gather.14.cloned.1.call-update) | async-done | bytes 2097168 | tf_op jit(solution)/shard_map/all_gather | solution.py:52
  228.6 2.7 reshape.58
  232.9 1.3 exponential_reduce_fusion
  234.4 18.0 all-reduce.4
  255.6 5.3 all-to-all-start
  261.0 4.3 fusion.11
  265.3 174.3 %all-gather.7 = f32[128,1,256]{2,1,0:T(1,128)S(1)} all-gather(f32[1,1,256]{2,1,0:T(1,128)S(1)} %bitcast.108), channel_id=2, replica_groups=mesh['tt'=8,'sv'=16] {'tt','sv'}, dimensions={0}, use_global_device_ids=true | all-gather | bytes 132096 | tf_op jit(solution)/shard_map/all_gather | solution.py:10
  441.3 62.2 %all-reduce.2 = f32[128]{0:T(128)} all-reduce(f32[128]{0:T(128)S(1)} %dynamic-update-slice.2), channel_id=1, replica_groups=mesh['tt'=8,'sv'=16] {'tt','sv'}, use_global_device_ids=true, to_apply=%add.2 | all-reduce | flops 128 | bytes 1024
  503.5 1.3 slice.63
  504.8 1.4 fusion.6
  506.2 173.5 %all-gather.8 = f32[128,1,256]{2,1,0:T(1,128)S(1)} all-gather(f32[1,1,256]{2,1,0:T(1,128)S(1)} %bitcast.111), channel_id=3, replica_groups=mesh['tt'=8,'sv'=16] {'tt','sv'}, dimensions={0}, use_global_device_ids=true | all-gather | bytes 132096 | tf_op jit(solution)/shard_map/all_gather | solution.py:10
  680.3 170.6 %all-gather.9 = f32[128,1,256]{2,1,0:T(1,128)S(1)} all-gather(f32[1,1,256]{2,1,0:T(1,128)S(1)} %bitcast.110), channel_id=6, replica_groups=mesh['tt'=8,'sv'=16] {'tt','sv'}, dimensions={0}, use_global_device_ids=true | all-gather | bytes 132096 | tf_op jit(solution)/shard_map/all_gather | solution.py:10
  851.1 172.1 %all-gather.10 = f32[128,1,256]{2,1,0:T(1,128)S(1)} all-gather(f32[1,1,256]{2,1,0:T(1,128)S(1)} %reshape.65), channel_id=1, replica_groups=mesh['tt'=8,'sv'=16] {'tt','sv'}, dimensions={0}, use_global_device_ids=true | all-gather | bytes 132096 | tf_op jit(solution)/shard_map/all_gather | solution.py:10
  1023.3 170.6 %all-gather.11 = f32[128,1,256]{2,1,0:T(1,128)S(1)} all-gather(f32[1,1,256]{2,1,0:T(1,128)S(1)} %bitcast.109), channel_id=7, replica_groups=mesh['tt'=8,'sv'=16] {'tt','sv'}, dimensions={0}, use_global_device_ids=true | all-gather | bytes 132096 | tf_op jit(solution)/shard_map/all_gather | solution.py:10
  1194.0 558.2 %while.33 = (s32[]{:T(128)}, f32[256]{0:T(256)S(1)}, f32[256]{0:T(256)}, f32[256]{0:T(256)S(1)}, f32[256]{0:T(256)S(1)}, /*index=5*/f32[256]{0:T(256)S(1)}, f32[...) while((s32[]{:T(128)}, f32[256]{0:T(256)S(1)}, ...), condition=%wide.region_12.13_spmd, body=%wide.region_11.12_spmd.sunk | while | flops 2307 | bytes 25777 | solution.py:13
  1194.0 1.3 multiply_add_fusion.2
  1198.4 1.3 multiply_add_fusion.2
  1202.8 1.3 multiply_add_fusion.2
  1211.6 1.3 multiply_add_fusion.2
  1216.0 1.3 multiply_add_fusion.2
  1220.4 1.3 multiply_add_fusion.2
  1224.8 1.3 multiply_add_fusion.2
  1229.2 1.3 multiply_add_fusion.2
  1238.0 1.3 multiply_add_fusion.2
  1242.4 1.3 multiply_add_fusion.2
  1246.8 1.3 multiply_add_fusion.2
  1251.2 1.3 multiply_add_fusion.2
  1255.6 1.3 multiply_add_fusion.2
  1264.3 1.3 multiply_add_fusion.2
  1268.7 1.3 multiply_add_fusion.2
  1273.1 1.3 multiply_add_fusion.2
  1277.5 1.3 multiply_add_fusion.2
  1281.9 1.3 multiply_add_fusion.2
  1286.3 1.3 multiply_add_fusion.2
  1295.1 1.3 multiply_add_fusion.2
  1299.5 1.3 multiply_add_fusion.2
  1303.9 1.3 multiply_add_fusion.2
  1308.3 1.3 multiply_add_fusion.2
  1312.7 1.3 multiply_add_fusion.2
  1321.5 1.3 multiply_add_fusion.2
  1325.9 1.3 multiply_add_fusion.2
  1330.3 1.3 multiply_add_fusion.2
  1334.7 1.3 multiply_add_fusion.2
  1339.1 1.3 multiply_add_fusion.2
  1347.9 1.3 multiply_add_fusion.2
  1352.3 1.3 multiply_add_fusion.2
  1356.7 1.3 multiply_add_fusion.2
  1361.0 1.3 multiply_add_fusion.2
  1365.4 1.3 multiply_add_fusion.2
  1369.8 1.3 multiply_add_fusion.2
  1378.6 1.3 multiply_add_fusion.2
  1383.0 1.3 multiply_add_fusion.2
  1387.4 1.3 multiply_add_fusion.2
  1391.8 1.3 multiply_add_fusion.2
  1396.2 1.3 multiply_add_fusion.2
  1405.0 1.3 multiply_add_fusion.2
  1752.2 1.3 subtract_reduce_fusion
  1753.5 1.3 fusion.8
  1754.8 5.4 fusion.13
  1760.3 3.3 fusion.5
  1763.6 6.4 copy.11
  1771.9 137.6 %all-reduce.7.cloned.1.call-done = f32[256,4096]{1,0:T(8,128)} async-done(((f32[256,4096]{1,0:T(8,128)}), f32[256,4096]{1,0:T(8,128)}) %all-reduce.7.cloned.1.call-update) | async-done | bytes 4194320
  1909.5 1.5 constant_dynamic-slice_fusion.7
  (1043 shorter events, 284.9 us)
Async XLA Ops:
  8.0 1.0 copy-start
  8.0 220.6 %all-gather.14.cloned.1.call-start = ((), (), s32[]{:S(2)}) async-start(), calls=%async_computation.3 | async-start | bytes 2113536 | tf_op jit(solution)/shard_map/all_gather | solution.py:52
  8.7 222.7 %reduce-scatter.2.cloned.1.call-start = ((), (), s32[]{:S(2)}) async-start(), calls=%async_computation.2 | async-start | bytes 8912896 | tf_op jit(solution)/shard_map/reduce_scatter | solution.py:39
  21.5 0.7 copy-start.8
  23.4 481.4 %copy-start.4 = (s32[512]{0:T(512)}, s32[512]{0:T(512)S(1)}, u32[]{:S(2)}) copy-start(s32[512]{0:T(512)S(1)} %iota_add_fusion) | copy-start | bytes 6148
  253.0 2.6 copy-start.6
  254.2 0.7 copy-start.2
  255.6 249.2 %all-to-all-start = ((bf16[16,16,512]{2,0,1:T(8,128)(2,1)}), bf16[16,16,512]{2,0,1:T(8,128)(2,1)S(1)}, u32[]{:S(2)}, u32[]{:S(2)}) async-start(bf16[16,16,512]{2,0,1:T(8,128)(2,1)} %bitcast.65), calls=%async_computation.1 | async-start | bytes 524288 | tf_op jit(solution)/shard_map/all_to_all | solution.py:51
  260.9 178.7 %copy-start.1 = (f32[16,8192]{1,0:T(8,128)S(1)}, f32[16,8192]{1,0:T(8,128)}, u32[]{:S(2)}) copy-start(f32[16,8192]{1,0:T(8,128)} %reduce-scatter.2.cloned.1.call-done) | copy-start | bytes 1572868
  260.9 243.8 %copy-start.5 = (s32[256]{0:T(256)S(1)}, s32[256]{0:T(256)}, u32[]{:S(2)}) copy-start(s32[256]{0:T(256)} %param.13) | copy-start | bytes 3076
  261.0 1648.6 %all-reduce.7.cloned.1.call-start = ((), (), s32[]{:S(2)}) async-start(), calls=%async_computation.4 | async-start | bytes 8388608
  261.0 178.6 %copy-start.3 = (bf16[16,8192]{1,0:T(8,128)(2,1)S(1)}, bf16[16,8192]{1,0:T(8,128)(2,1)}, u32[]{:S(2)}) copy-start(bf16[16,8192]{1,0:T(8,128)(2,1)} %copy-done.2) | copy-start | bytes 786436
  261.0 178.6 %copy-start.7 = (f32[16]{0:T(128)S(1)}, f32[16]{0:T(128)}, u32[]{:S(2)}) copy-start(f32[16]{0:T(128)} %copy-done.6) | copy-start | bytes 196
Sparse Core Ops, SparseCore 0:
  10.6 218.0 all-gather.13
  1760.4 149.0 all-reduce.6
Sparse Core Ops, SparseCore 1:
  21.6 104.9 reduce-scatter.1
where the time goes:
time: 1930 us; the launch traced here: 1920 us
  blocking collectives  941 us (49%)
  waiting for transfers between devices  344 us (18%)
  loops' own time  231 us (12%)
  local copies, waits for them, and re-layouts  178 us (9%)
  other arithmetic  176 us (9%)
  matrix products  25.4 us (1%)
  between operations  19.4 us (1%)
    all_gather x5, blocking collectives, merged(): pieces = jax.tree.map(lambda part: lax.all_gather(part, axis), value)  861 us
    another operation x2, loops' own time, merged(): lax.scan(lambda total, piece: (join(total, piece), None), head, tail)  231 us
    all_gather x1, waiting for transfers between devices, body(): lax.all_gather(student_hidden, ('tt', 'sv'), axis=0, tiled=True)  205 us
    add x134, other arithmetic, combine_pair(): first[1] * jnp.exp(first[0] - top) + second[1] * jnp.exp(second[0] - top)  163 us
    dynamic_slice x508, local copies, waits for them, and re-layouts, merged(): lax.scan(lambda total, piece: (join(total, piece), None), head, tail)  161 us
    unnamed x4, waiting for transfers between devices  138 us
    unnamed x2, blocking collectives  80.2 us
  transfers between devices with their start and end apart: 4, of which 2 were waited for; matrix products, arithmetic and copies ran while one was open for 2% of the time, Pallas kernels for 0%

commit v1 on v0

v1 whole, which is shorter than its diff:
```python
import jax
import jax.numpy as jnp
from jax import lax
from jax.experimental import pallas as pl
from jax.experimental.pallas import tpu as pltpu
from jax.sharding import Mesh, PartitionSpec as P

ce_weight = 0.5
f16, f32, bf16, i16 = jnp.float16, jnp.float32, jnp.bfloat16, jnp.int16
axes = ("zl", "x", "zh", "y", "c")
sizes = (2, 4, 2, 4, 2)
grad_scale = 4096.0


def shift(value, axis, step):
    size = sizes[axes.index(axis)]
    return lax.ppermute(value, axis, [((i + step) % size, i) for i in range(size)])


def send(value, axis, step):
    size = sizes[axes.index(axis)]
    return lax.ppermute(value, axis, [(i, (i + step) % size) for i in range(size)])


def cross_z(value, across):
    pairs = [(i, i ^ (2 * ("zl" in across) + ("zh" in across))) for i in range(4)]
    return lax.ppermute(value, ("zl", "zh"), pairs)


def ring_pair(axis, first):
    return [(0, 1), (1, 0), (2, 3), (3, 2)] if first else [(0, 3), (3, 0), (1, 2), (2, 1)]


def merge(a, b):
    top_t = jnp.maximum(a[0], b[0])
    top_s = jnp.maximum(a[4], b[4])
    at, bt = jnp.exp(a[0] - top_t), jnp.exp(b[0] - top_t)
    as_, bs = jnp.exp(a[4] - top_s), jnp.exp(b[4] - top_s)
    return jnp.stack(
        [
            top_t,
            a[1] * at + b[1] * bt,
            a[2] * at + b[2] * bt,
            a[3] * at + b[3] * bt,
            top_s,
            a[5] * as_ + b[5] * bs,
            a[6] + b[6],
            a[7] + b[7],
        ]
    )


def merge_all(stats):
    stats = merge(stats, send(stats, "c", 1))
    for axis in ("x", "y"):
        for first in (True, False):
            stats = merge(stats, lax.ppermute(stats, axis, ring_pair(axis, first)))
    one, two, three = [cross_z(stats, r) for r in (("zl",), ("zh",), ("zl", "zh"))]
    return merge(merge(stats, one), merge(two, three))


def row_code(top):
    return jnp.ceil(8.0 * jnp.log2(jnp.maximum(top, 1e-30)) + 0.01)


def step_of(code):
    return jnp.exp2(code * 0.125) * (1.0 / 32000.0)


def top_of(blocks):
    top = jnp.max(jnp.abs(blocks[0]), axis=1, keepdims=True)
    for block in blocks[1:]:
        top = jnp.maximum(top, jnp.max(jnp.abs(block), axis=1, keepdims=True))
    return top


def put(ref, blocks, code):
    inverse = 1.0 / step_of(code)
    for i, block in enumerate(blocks):
        ref[:, i * 512 : (i + 1) * 512] = jnp.round(block * inverse).astype(i16)
    n = len(blocks) * 512
    ref[:, n : n + 128] = jnp.broadcast_to(code, (code.shape[0], 128)).astype(i16)


def take(ref, i, count):
    step = step_of(ref[:, count * 512 : count * 512 + 128].astype(f32)[:, :1])
    return ref[:, i * 512 : (i + 1) * 512].astype(f32) * step


def cost(us):
    return pl.CostEstimate(flops=int(us * 1e9), bytes_accessed=int(us * 2.5e6), transcendentals=0)


anywhere = pl.BlockSpec(memory_space=pl.ANY)
in_vmem = pl.BlockSpec(memory_space=pltpu.VMEM)
in_smem = pl.BlockSpec(memory_space=pltpu.SMEM)


def fetch_blocks(order_ref, head_ref, held, sems):
    copies = []
    for j in range(held.shape[0]):
        columns = pl.ds(pl.multiple_of(order_ref[j] * 512, 512), 512)
        copies.append(pltpu.make_async_copy(head_ref.at[:, columns], held.at[j], sems.at[j]))
        copies[-1].start()
    return copies


def far_products(hidden, head, order):
    count = order.shape[0]
    rows, depth = hidden.shape

    def kernel(order_ref, hidden_ref, head_ref, out_ref, held, sems):
        copies = fetch_blocks(order_ref, head_ref, held, sems)
        for j in range(count):
            copies[j].wait()
            block = jnp.dot(hidden_ref[...], held[j], preferred_element_type=f32)
            put(out_ref.at[j], [block], row_code(top_of([block])))

    return pl.pallas_call(
        kernel,
        in_specs=[in_smem, in_vmem, anywhere],
        out_specs=in_vmem,
        out_shape=jax.ShapeDtypeStruct((count, rows, 640), i16),
        scratch_shapes=[pltpu.VMEM((count, depth, 512), bf16), pltpu.SemaphoreType.DMA((count,))],
        compiler_params=pltpu.CompilerParams(vmem_limit_bytes=50 << 20),
        cost_estimate=cost(6),
    )(order, hidden, head)


def first_products(hidden, head, order):
    count = order.shape[0]
    rows, depth = hidden.shape

    def kernel(order_ref, hidden_ref, head_ref, out_ref, held, sems):
        copies = fetch_blocks(order_ref, head_ref, held, sems)
        for j in range(count):
            copies[j].wait()
            out_ref[j] = jnp.dot(hidden_ref[...], held[j], preferred_element_type=f32)

    return pl.pallas_call(
        kernel,
        in_specs=[in_smem, in_vmem, anywhere],
        out_specs=in_vmem,
        out_shape=jax.ShapeDtypeStruct((count, rows, 512), f32),
        scratch_shapes=[pltpu.VMEM((count, depth, 512), bf16), pltpu.SemaphoreType.DMA((count,))],
        compiler_params=pltpu.CompilerParams(vmem_limit_bytes=50 << 20),
        cost_estimate=cost(4),
    )(order, hidden, head)


def own_products(hidden, head, order, first, other, ready):
    rows, depth = hidden.shape
    half = rows // 2

    def kernel(order_ref, hidden_ref, head_ref, first_ref, other_ref, *refs):
        a1, a2, a3, b1, keep_a, keep_b, held, sums, sems = refs[len(ready) :]
        copies = fetch_blocks(order_ref, head_ref, held, sems)
        up, low = jnp.zeros((half, 1), f32), jnp.zeros((half, 1), f32)
        for j in range(8):
            if j < 4:
                block = first_ref[j]
            else:
                copies[j - 4].wait()
                block = jnp.dot(hidden_ref[...], held[j - 4], preferred_element_type=f32)
            block += take(other_ref.at[j], 0, 1)
            top = jnp.max(jnp.abs(block), axis=1, keepdims=True)
            if j % 4:
                sums[j, :half] = block[:half]
                up = jnp.maximum(up, top[:half])
            else:
                keep_a[:, j * 128 : j * 128 + 512] = block[:half]
            if j >= 4:
                sums[j, half:] = block[half:]
                low = jnp.maximum(low, top[half:])
            else:
                keep_b[:, j * 512 : j * 512 + 512] = block[half:]
        code = row_code(up)
        for d, ref in ((1, a1), (2, a2), (3, a3)):
            put(ref, [sums[d, :half], sums[4 + d, :half]], code)
        put(b1, [sums[4 + d, half:] for d in range(4)], row_code(low))

    outs = [(half, 1152, i16)] * 3 + [(half, 2176, i16), (half, 1024, f32), (half, 2048, f32)]
    return pl.pallas_call(
        kernel,
        in_specs=[in_smem, in_vmem, anywhere, in_vmem, in_vmem] + [anywhere] * len(ready),
        out_specs=[in_vmem] * len(outs),
        out_shape=[jax.ShapeDtypeStruct((m, n), d) for m, n, d in outs],
        scratch_shapes=[
            pltpu.VMEM((4, depth, 512), bf16),
            pltpu.VMEM((8, rows, 512), f32),
            pltpu.SemaphoreType.DMA((4,)),
        ],
        compiler_params=pltpu.CompilerParams(vmem_limit_bytes=50 << 20),
        cost_estimate=cost(7),
    )(order, hidden, head, first, other, *ready)


def whole_call(kernel, ins, outs, ready=(), scratch=(), us=0.5):
    total = sum(a.size * a.dtype.itemsize for a in ins)
    return pl.pallas_call(
        kernel,
        in_specs=[in_vmem] * len(ins) + [anywhere] * len(ready),
        out_specs=[in_vmem] * len(outs),
        out_shape=[jax.ShapeDtypeStruct(tuple(shape), d) for *shape, d in outs],
        scratch_shapes=scratch,
        compiler_params=pltpu.CompilerParams(vmem_limit_bytes=16 << 20),
        cost_estimate=cost(us),
    )(*ins, *ready)


def lay_two(r0, r1, r2, r3, out, wide):
    for i, ref in enumerate((r0, r1, r2, r3)):
        wide[2 * i : 2 * i + 2] = ref[...].astype(f32)
    out[...] = wide[...].astype(bf16)


def lay(*refs):
    *ins, out = refs
    count = out.shape[0] // ins[0].shape[0]
    out[...] = jnp.concatenate([r[...].astype(f32) for r in ins[:count]], axis=0).astype(bf16)


def split_second(keep_a, r1, r2, r3, keep_b, rz, a1, b1, b2, b3, out_a, out_b):
    mine, other = [
        keep_a[:, i * 512 : (i + 1) * 512] + take(r1, i, 2) + take(r2, i, 2) + take(r3, i, 2)
        for i in range(2)
    ]
    out_a[...] = mine
    put(a1, [other], row_code(top_of([other])))
    low = [keep_b[:, d * 512 : (d + 1) * 512] + take(rz, d, 4) for d in range(4)]
    out_b[...] = low[0]
    code = row_code(top_of(low[1:]))
    for d, ref in ((1, b1), (2, b2), (3, b3)):
        put(ref, [low[d]], code)


def join_last(keep_a, rz, keep_b, r1, r2, r3, _, out_a, out_b):
    out_a[...] = keep_a[...] + take(rz, 0, 1)
    out_b[...] = keep_b[...] + take(r1, 0, 1) + take(r2, 0, 1) + take(r3, 0, 1)


def token_order(me):
    zl, x, zh, y, c = me
    r = lax.iota(jnp.int32, 256)
    t, i, j, dy, dx, k = r % 2, (r // 2) % 2, (r // 4) % 2, (r // 8) % 4, (r // 32) % 4, r // 128
    zl_, zh_, y_, x_, c_ = (zl + i) % 2, (zh + j) % 2, (y + dy) % 4, (x + dx) % 4, (c + k) % 2
    return ((((zl_ * 4 + x_) * 2 + zh_) * 4 + y_) * 2 + c_) * 2 + t


def gathered_order(me):
    zl, x, zh, y, c = me
    r = lax.iota(jnp.int32, 256)
    t, i, j, dy, dx, k = r % 2, (r // 2) % 2, (r // 4) % 2, (r // 8) % 4, (r // 32) % 4, r // 128
    zl_, zh_, y_, c_ = (zl + i) % 2, (zh + j) % 2, (y + dy) % 4, (c + k) % 2
    x_ = jnp.bitwise_xor(x, jnp.bitwise_xor(dx, dx // 2))
    return ((((zl_ * 4 + x_) * 2 + zh_) * 4 + y_) * 2 + c_) * 2 + t


def placing(order):
    n = order.shape[0]
    return (lax.broadcasted_iota(jnp.int32, (n, n), 0) == order[None, :]).astype(bf16)


def grad_rows(grad, head):
    feats, depth = head.shape
    steps = 8
    wide = feats // steps

    def kernel(grad_ref, head_ref, far_ref, near_ref, held, sems):
        copies = []
        for j in range(steps):
            part = head_ref.at[pl.ds(j * wide, wide), :]
            copies.append(pltpu.make_async_copy(part, held.at[j], sems.at[j]))
            copies[-1].start()
        for j in range(steps):
            copies[j].wait()
            both = lax.dot_general(
                grad_ref[...], held[j], (((1,), (1,)), ((), ())), preferred_element_type=f32
            )
            near_ref[:, j * wide : (j + 1) * wide] = both[:128]
            far_ref[:, j * wide : (j + 1) * wide] = both[128:]

    return pl.pallas_call(
        kernel,
        in_specs=[in_vmem, anywhere],
        out_specs=[in_vmem] * 2,
        out_shape=[jax.ShapeDtypeStruct((128, feats), f32)] * 2,
        scratch_shapes=[pltpu.VMEM((steps, wide, depth), bf16), pltpu.SemaphoreType.DMA((steps,))],
        compiler_params=pltpu.CompilerParams(vmem_limit_bytes=50 << 20),
        cost_estimate=cost(4),
    )(grad, head)


def scatter_rows(far, near):
    total = near + send((far * grad_scale).astype(f16), "c", 1).astype(f32) * (1.0 / grad_scale)
    out = (total * grad_scale).astype(f16).reshape(4, 32, -1)
    got = [send(out[d], "x", d) for d in (1, 2, 3)]
    total = total[:32] + sum(g.astype(f32) for g in got) * (1.0 / grad_scale)
    out = (total * grad_scale).astype(f16).reshape(4, 8, -1)
    got = [send(out[d], "y", d) for d in (1, 2, 3)]
    total = total[:8] + sum(g.astype(f32) for g in got) * (1.0 / grad_scale)
    across = ((1, ("zl",)), (2, ("zh",)), (3, ("zl", "zh")))
    return total[:2] + sum(cross_z(total[2 * i : 2 * i + 2], r) for i, r in across)


def body(teacher_hidden, teacher_head, student_hidden, student_head, targets):
    tokens = teacher_hidden.shape[0]
    vocab_dev = student_head.shape[1]
    me = tuple(lax.axis_index(a) for a in axes)
    zl, x, zh, y, c = me
    j = jnp.arange(8, dtype=jnp.int32)
    column = (((zh + j // 4) % 2) * 4 + (y + j % 4) % 4) * 2

    ring = [("zl",), ("zh",), ("zl", "zh")]
    rows = [student_hidden] + [cross_z(student_hidden, r) for r in ring]
    (rows,) = whole_call(lay_two, rows, [(8, 4096, bf16)], scratch=[pltpu.VMEM((8, 4096), f32)])
    rows = [rows] + [shift(rows, "y", i) for i in (1, 2, 3)]
    (rows,) = whole_call(lay, rows, [(32, 4096, bf16)], us=80)
    paired = lax.ppermute(rows, "x", ring_pair("x", True))
    other = far_products(teacher_hidden, teacher_head, column + 1 - c)
    other = send(other, "c", 1)
    first = first_products(teacher_hidden, teacher_head, column[:4] + c)
    a1, a2, a3, b1, keep_a, keep_b = own_products(
        teacher_hidden, teacher_head, column[4:] + c, first, other, [rows]
    )
    a1, a2, a3, b1 = send(a1, "y", 1), send(a2, "y", 2), send(a3, "y", 3), send(b1, "zh", 1)
    (rows,) = whole_call(lay, [rows, paired], [(64, 4096, bf16)], [keep_b])
    paired = lax.ppermute(rows, "x", ring_pair("x", False))
    a1, b1, b2, b3, keep_a, keep_b = whole_call(
        split_second,
        [keep_a, a1, a2, a3, keep_b, b1],
        [(128, 640, i16)] * 4 + [(128, 512, f32)] * 2,
    )
    a1, b1, b2, b3 = send(a1, "zh", 1), send(b1, "y", 1), send(b2, "y", 2), send(b3, "y", 3)

    (rows,) = whole_call(lay, [rows, paired], [(128, 4096, bf16)], [keep_a])
    gathered = jnp.concatenate([rows, shift(rows, "c", 1)], axis=0)
    place = placing(gathered_order(me))
    hidden_all = jnp.dot(place, gathered, preferred_element_type=f32).astype(bf16)
    logits_s = jnp.dot(hidden_all, student_head, preferred_element_type=f32)
    logits_t = whole_call(
        join_last, [keep_a, a1, keep_b, b1, b2, b3], [(128, 512, f32)] * 2, [logits_s]
    )
    logits_t = jnp.concatenate(logits_t, axis=0)

    offset = lax.axis_index(axes) * vocab_dev
    columns = offset + lax.broadcasted_iota(jnp.int32, (1, vocab_dev), 1)
    hit = (columns == targets[:, None]).astype(f32)
    top_t = jnp.max(logits_t, axis=1)
    exp_t = jnp.exp(logits_t - top_t[:, None])
    top_s = jnp.max(logits_s, axis=1)
    stats = jnp.stack(
        [
            top_t,
            jnp.sum(exp_t, axis=1),
            jnp.sum(exp_t * logits_s, axis=1),
            jnp.sum(exp_t * logits_t, axis=1),
            top_s,
            jnp.sum(jnp.exp(logits_s - top_s[:, None]), axis=1),
            jnp.sum(hit * logits_s, axis=1),
            jnp.zeros((tokens,), f32),
        ]
    )
    stats = merge_all(stats)
    norm_t = stats[0] + jnp.log(stats[1])
    norm_s = stats[4] + jnp.log(stats[5])
    mass = stats[1] / stats[1]
    cross = stats[2] / stats[1]
    entropy = stats[3] / stats[1] - mass * norm_t
    loss = jnp.sum(entropy - (cross - mass * norm_s) + ce_weight * (norm_s - stats[6])) / tokens

    probs = jnp.exp(logits_t - norm_t[:, None]).astype(bf16).astype(f32)
    probs_s = jnp.exp(logits_s - norm_s[:, None])
    grad_logits = ((mass + ce_weight)[:, None] * probs_s - probs - ce_weight * hit).astype(bf16)
    head_grad = lax.dot_general(
        hidden_all, grad_logits, (((0,), (0,)), ((), ())), preferred_element_type=f32
    ).astype(bf16)
    sorted_grad = lax.dot_general(
        placing(token_order(me)), grad_logits, (((0,), (0,)), ((), ())), preferred_element_type=f32
    ).astype(bf16)
    hidden_grad = scatter_rows(*grad_rows(sorted_grad, student_head))
    return (loss, head_grad, hidden_grad)


def solution(mesh):
    fine = Mesh(mesh.devices.reshape(sizes), axes)
    tt, sv = ("zl", "x"), ("zh", "y", "c")
    placed = (P(None, sv), P(sv, tt), P(axes, None), P(None, axes), P())
    return jax.shard_map(
        body,
        mesh=fine,
        in_specs=placed,
        out_specs=(P(), P(None, axes), P(axes, None)),
        check_vma=False,
    )
```

time: 1930 us -> 144 us (0.07)
  blocking collectives: 941 us -> 0 us
  waiting for transfers between devices: 344 us -> 56.4 us
  loops' own time: 231 us -> 0 us
  local copies, waits for them, and re-layouts: 178 us -> 4.46 us
  other arithmetic: 176 us -> 3.39 us
  starting transfers between devices: 5.43 us -> 47.9 us
  Pallas kernels: 0 us -> 22.6 us
  matrix products: 25.4 us -> 5.68 us
    all_gather x5 -> x0, blocking collectives: 861 us -> none  [merged(): pieces = jax.tree.map(lambda part: lax.all_gather(part, axis), value)]
    another operation x2 -> x0, loops' own time: 231 us -> none  [merged(): lax.scan(lambda total, piece: (join(total, piece), None), head, tail)]
    all_gather x1 -> x0, waiting for transfers between devices: 205 us -> none  [body(): lax.all_gather(student_hidden, ('tt', 'sv'), axis=0, tiled=True)]
    add x516 -> x17, other arithmetic: 167 us -> 1.03 us  [the longest x1 0.65 us: scatter_rows(): total[:2] + sum((cross_z(total[2 * i:2 * i + 2], r) for i, r in across))]
    dynamic_slice x508 -> x0, local copies, waits for them, and re-layouts: 161 us -> none  [merged(): lax.scan(lambda total, piece: (join(total, piece), None), head, tail)]
    unnamed x4 -> x0, waiting for transfers between devices: 138 us -> none
    unnamed x2 -> x0, blocking collectives: 80.2 us -> none
    ppermute x0 -> x36, waiting for transfers between devices: none -> 56.4 us  [the longest x17 37.1 us: send(): lax.ppermute(value, axis, [(i, (i + step) % size) for i in range(size)])]
  transfers between devices with their start and end apart: 4 -> 36, of which waited for: 2 -> 18; matrix products, arithmetic and copies ran while one was open for 2% -> 4% of each run, Pallas kernels for 0% -> 12%
where the time goes in v1:
time: 144 us; the launch traced here: 143 us
  waiting for transfers between devices  56.4 us (39%)
  starting transfers between devices  47.9 us (33%)
  Pallas kernels  22.6 us (16%)
  matrix products  5.68 us (4%)
  local copies, waits for them, and re-layouts  4.46 us (3%)
  other arithmetic  3.39 us (2%)
  between operations  2.89 us (2%)
    ppermute x17, waiting for transfers between devices, send(): lax.ppermute(value, axis, [(i, (i + step) % size) for i in range(size)])  37.1 us
    ppermute x17, starting transfers between devices, send(): lax.ppermute(value, axis, [(i, (i + step) % size) for i in range(size)])  19.3 us
    ppermute x9, starting transfers between devices, cross_z(): return lax.ppermute(value, ('zl', 'zh'), pairs)  15.3 us
    ppermute x4, waiting for transfers between devices, merge_all(): stats = merge(stats, lax.ppermute(stats, axis, ring_pair(axis, first)))  12.6 us
    pallas_call x1, Pallas kernels, far_products(): pl.pallas_call(kernel, in_specs=[in_smem, in_vmem, anywhere], out_specs=i...  6.71 us
    pallas_call x1, Pallas kernels, own_products(): pl.pallas_call(kernel, in_specs=[in_smem, in_vmem, anywhere, in_vmem, in_...  6.17 us
    pallas_call x1, Pallas kernels, grad_rows(): pl.pallas_call(kernel, in_specs=[in_vmem, anywhere], out_specs=[in_vmem]...  5.09 us
    ppermute x9, waiting for transfers between devices, cross_z(): return lax.ppermute(value, ('zl', 'zh'), pairs)  4.86 us
  transfers between devices with their start and end apart: 36, of which 18 were waited for; matrix products, arithmetic and copies ran while one was open for 4% of the time, Pallas kernels for 12%

profile of v1, /device:TPU:0, one launch (start us, length us, event | category | flops | bytes accessed | tf_op | source)
XLA Modules:
  0.0 143.3 jit_solution(13150899876190323723)
XLA Ops:
  0.6 2.1 %collective-permute-start.1 = (bf16[2,4096]{1,0:T(2,128)(2,1)}, bf16[2,4096]{1,0:T(2,128)(2,1)S(1)}, u32[]{:S(2)}, u32[]{:S(2)}) collective-permute-start(bf16[2,4096]{1,0:T(2,128)(2,1)} %r0.1), channel_id=1, source_target_pairs={{0,64},{8,72},{64,0},{72,8},{1,65},{9,73},{65,1},{73,9},{2,66},{10... | collective-permute-start | bytes 49160 | tf_op jit(solution)/shard_map/ppermute | solution.py:27
  2.7 3.6 %collective-permute-start.2 = (bf16[2,4096]{1,0:T(2,128)(2,1)}, bf16[2,4096]{1,0:T(2,128)(2,1)S(1)}, u32[]{:S(2)}, u32[]{:S(2)}) collective-permute-start(bf16[2,4096]{1,0:T(2,128)(2,1)} %r0.1), channel_id=1, source_target_pairs={{0,8},{8,0},{64,72},{72,64},{1,9},{9,1},{65,73},{73,65},{2,10},{10... | collective-permute-start | bytes 49160 | tf_op jit(solution)/shard_map/ppermute | solution.py:27
  6.3 1.0 copy-done.1
  7.4 6.7 %shard_map.77 = s16[8,256,640]{2,1,0:T(8,128)(2,1)S(1)} custom-call(s32[8]{0:T(128)S(1)} %get-tuple-element.64.order_ref, bf16[256,1024]{1,0:T(8,128)(2,1)S(1)} %copy-done.1, bf16[1024,8192]{1,0:T(8,128)(2,1)} %head_ref.6), custom_call_target="tpu_custom_call" | custom-call | flops 6000000000 | bytes 15000000 | tf_op jit(solution)/shard_map/pallas_call | solution.py:119
  14.3 3.1 %collective-permute-start.4 = (bf16[8,4096]{1,0:T(8,128)(2,1)S(1)}, bf16[8,4096]{1,0:T(8,128)(2,1)S(1)}, u32[]{:S(2)}, u32[]{:S(2)}) collective-permute-start(bf16[8,4096]{1,0:T(8,128)(2,1)S(1)} %shard_map.78.refs_0_), channel_id=1, source_target_pairs={{2,0},{4,2},{6,4},{0,6},{3,1},{5,3},{7,5},{1,7},{10,8},{12,10},{14... | collective-permute-start | bytes 196616 | tf_op jit(solution)/shard_map/ppermute | solution.py:17
  17.4 0.6 collective-permute-start.5
  18.0 1.0 collective-permute-start.6
  19.0 3.6 %shard_map.76.first_ref = f32[4,256,512]{2,1,0:T(8,128)S(1)} custom-call(s32[4]{0:T(128)S(1)} %get-tuple-element.198.order_ref, bf16[256,1024]{1,0:T(8,128)(2,1)S(1)} %copy-done.2, bf16[1024,8192]{1,0:T(8,128)(2,1)} %head_ref.6), custom_call_target="tpu_custom_call" | custom-call | flops 4000000000 | bytes 10000000 | tf_op jit(solution)/shard_map/pallas_call | solution.py:140
  22.6 1.2 collective-permute-done.5.refs_2_
  23.8 0.7 collective-permute-done.6.refs_3_
  24.6 1.6 %collective-permute-start.15 = (bf16[32,4096]{1,0:T(8,128)(2,1)S(1)}, bf16[32,4096]{1,0:T(8,128)(2,1)S(1)}, u32[]{:S(2)}, u32[]{:S(2)}) collective-permute-start(bf16[32,4096]{1,0:T(8,128)(2,1)S(1)} %shard_map.79.refs_0_), channel_id=1, source_target_pairs={{0,16},{16,0},{32,48},{48,32},{1,17},{17,1},{33,49},{49,33},{2,18}... | collective-permute-start | bytes 786440 | tf_op jit(solution)/shard_map/ppermute | solution.py:319
  26.1 1.5 %copy-done.9 = s16[8,256,640]{2,1,0:T(8,128)(2,1)} copy-done((s16[8,256,640]{2,1,0:T(8,128)(2,1)}, s16[8,256,640]{2,1,0:T(8,128)(2,1)S(1)}, u32[]{:S(2)}) %copy-start.9) | copy-done | bytes 2621464
  27.6 6.2 %shard_map.80 = (s16[128,1152]{1,0:T(8,128)(2,1)S(1)}, s16[128,1152]{1,0:T(8,128)(2,1)S(1)}, s16[128,1152]{1,0:T(8,128)(2,1)S(1)}, s16[128,2176]{1,0:T(8,128)(2,...) custom-call(s32[4]{0:T(128)S(1)} %get-tuple-element.199.order_ref, bf16[256,1024]{1,0:T(8,128)(2,1)S(1)} %copy-done.2, ...), custom_call_target="tpu_custom_call" | custom-call | flops 7000000000 | bytes 17500000 | tf_op jit(solution)/shard_map/pallas_call | solution.py:183
  33.8 1.9 %collective-permute-start.10 = (s16[128,2176]{1,0:T(8,128)(2,1)S(1)}, s16[128,2176]{1,0:T(8,128)(2,1)S(1)}, u32[]{:S(2)}, u32[]{:S(2)}) collective-permute-start(s16[128,2176]{1,0:T(8,128)(2,1)S(1)} %get-tuple-element.24), channel_id=1, source_target_pairs={{0,8},{8,0},{1,9},{9,1},{2,10},{10,2},{3,11},{11,3},{4,12},{12,4},... | collective-permute-start | bytes 1671176 | tf_op jit(solution)/shard_map/ppermute | solution.py:22
  35.8 2.2 %collective-permute-start.16 = (bf16[64,4096]{1,0:T(8,128)(2,1)S(1)}, bf16[64,4096]{1,0:T(8,128)(2,1)S(1)}, u32[]{:S(2)}, u32[]{:S(2)}) collective-permute-start(bf16[64,4096]{1,0:T(8,128)(2,1)S(1)} %shard_map.82.refs_0_), channel_id=1, source_target_pairs={{0,48},{48,0},{16,32},{32,16},{1,49},{49,1},{17,33},{33,17},{2,50}... | collective-permute-start | bytes 1572872 | tf_op jit(solution)/shard_map/ppermute | solution.py:328
  38.0 1.2 collective-permute-start.7
  39.1 1.8 %collective-permute-start.8 = (s16[128,1152]{1,0:T(8,128)(2,1)S(1)}, s16[128,1152]{1,0:T(8,128)(2,1)S(1)}, u32[]{:S(2)}, u32[]{:S(2)}) collective-permute-start(s16[128,1152]{1,0:T(8,128)(2,1)S(1)} %get-tuple-element.21), channel_id=1, source_target_pairs={{0,4},{2,6},{4,0},{6,2},{1,5},{3,7},{5,1},{7,3},{8,12},{10,14},{12... | collective-permute-start | bytes 884744 | tf_op jit(solution)/shard_map/ppermute | solution.py:22
  41.0 0.8 collective-permute-start.9
  41.8 11.7 %collective-permute-done.7.r1 = s16[128,1152]{1,0:T(8,128)(2,1)S(1)} collective-permute-done((s16[128,1152]{1,0:T(8,128)(2,1)S(1)}, s16[128,1152]{1,0:T(8,128)(2,1)S(1)}, u32[]{:S(2)}, u32[]{:S(2)}) %collective-permute-start.7) | collective-permute-done | bytes 294944 | tf_op jit(solution)/shard_map/ppermute | solution.py:22
  53.5 0.6 collective-permute-done.9.r3
  54.1 0.7 shard_map.81
  55.1 1.9 %collective-permute-start.11 = (s16[128,640]{1,0:T(8,128)(2,1)S(1)}, s16[128,640]{1,0:T(8,128)(2,1)S(1)}, u32[]{:S(2)}, u32[]{:S(2)}) collective-permute-start(s16[128,640]{1,0:T(8,128)(2,1)S(1)} %get-tuple-element.26), channel_id=1, source_target_pairs={{0,8},{8,0},{1,9},{9,1},{2,10},{10,2},{3,11},{11,3},{4,12},{12,4},... | collective-permute-start | bytes 491528 | tf_op jit(solution)/shard_map/ppermute | solution.py:22
  57.0 0.6 collective-permute-start.12
  57.6 3.5 %collective-permute-start.13 = (s16[128,640]{1,0:T(8,128)(2,1)S(1)}, s16[128,640]{1,0:T(8,128)(2,1)S(1)}, u32[]{:S(2)}, u32[]{:S(2)}) collective-permute-start(s16[128,640]{1,0:T(8,128)(2,1)S(1)} %get-tuple-element.29), channel_id=1, source_target_pairs={{0,4},{2,6},{4,0},{6,2},{1,5},{3,7},{5,1},{7,3},{8,12},{10,14},{12... | collective-permute-start | bytes 491528 | tf_op jit(solution)/shard_map/ppermute | solution.py:22
  61.1 0.7 convolution_convert_fusion.1
  61.8 1.5 %copy-done.8 = bf16[4096,512]{1,0:T(8,128)(2,1)S(1)} copy-done((bf16[4096,512]{1,0:T(8,128)(2,1)S(1)}, bf16[4096,512]{1,0:T(8,128)(2,1)}, u32[]{:S(2)}) %copy-start.8) | copy-done | bytes 4194328
  63.3 1.4 fusion.59
  64.7 4.2 %collective-permute-done.13.r2 = s16[128,640]{1,0:T(8,128)(2,1)S(1)} collective-permute-done((s16[128,640]{1,0:T(8,128)(2,1)S(1)}, s16[128,640]{1,0:T(8,128)(2,1)S(1)}, u32[]{:S(2)}, u32[]{:S(2)}) %collective-permute-start.13) | collective-permute-done | bytes 163872 | tf_op jit(solution)/shard_map/ppermute | solution.py:22
  68.9 0.2 shard_map.84
  69.3 0.5 multiply_reduce_fusion.1
  69.9 1.2 collective-permute-done.18
  71.1 0.7 collective-permute-start.19
  71.8 3.1 %collective-permute-done.19 = f32[8,256]{1,0:T(8,128)S(1)} collective-permute-done((f32[8,256]{1,0:T(8,128)S(1)}, f32[8,256]{1,0:T(8,128)S(1)}, u32[]{:S(2)}, u32[]{:S(2)}) %collective-permute-start.19) | collective-permute-done | bytes 8224 | tf_op jit(solution)/shard_map/ppermute | solution.py:57
  74.9 1.2 collective-permute-start.20
  76.1 3.7 %collective-permute-done.20 = f32[8,256]{1,0:T(8,128)S(1)} collective-permute-done((f32[8,256]{1,0:T(8,128)S(1)}, f32[8,256]{1,0:T(8,128)S(1)}, u32[]{:S(2)}, u32[]{:S(2)}) %collective-permute-start.20) | collective-permute-done | bytes 8224 | tf_op jit(solution)/shard_map/ppermute | solution.py:57
  79.9 0.4 collective-permute-start.21
  80.3 3.3 %collective-permute-done.21 = f32[8,256]{1,0:T(8,128)S(1)} collective-permute-done((f32[8,256]{1,0:T(8,128)S(1)}, f32[8,256]{1,0:T(8,128)S(1)}, u32[]{:S(2)}, u32[]{:S(2)}) %collective-permute-start.21) | collective-permute-done | bytes 8224 | tf_op jit(solution)/shard_map/ppermute | solution.py:57
  83.7 2.5 %collective-permute-start.22 = (f32[8,256]{1,0:T(8,128)S(1)}, f32[8,256]{1,0:T(8,128)S(1)}, u32[]{:S(2)}, u32[]{:S(2)}) collective-permute-start(f32[8,256]{1,0:T(8,128)S(1)} %stack.37), channel_id=1, source_target_pairs={{0,6},{6,0},{2,4},{4,2},{1,7},{7,1},{3,5},{5,3},{8,14},{14,8},{10,... | collective-permute-start | bytes 24584 | tf_op jit(solution)/shard_map/ppermute | solution.py:57
  86.2 2.5 %collective-permute-done.22 = f32[8,256]{1,0:T(8,128)S(1)} collective-permute-done((f32[8,256]{1,0:T(8,128)S(1)}, f32[8,256]{1,0:T(8,128)S(1)}, u32[]{:S(2)}, u32[]{:S(2)}) %collective-permute-start.22) | collective-permute-done | bytes 8224 | tf_op jit(solution)/shard_map/ppermute | solution.py:57
  88.7 1.0 collective-permute-start.23
  89.8 3.9 %collective-permute-start.24 = (f32[8,256]{1,0:T(8,128)S(1)}, f32[8,256]{1,0:T(8,128)S(1)}, u32[]{:S(2)}, u32[]{:S(2)}) collective-permute-start(f32[8,256]{1,0:T(8,128)S(1)} %stack.38), channel_id=1, source_target_pairs={{0,8},{8,0},{64,72},{72,64},{1,9},{9,1},{65,73},{73,65},{2,10},{10... | collective-permute-start | bytes 24584 | tf_op jit(solution)/shard_map/ppermute | solution.py:27
  93.6 1.6 %collective-permute-done.24 = f32[8,256]{1,0:T(8,128)S(1)} collective-permute-done((f32[8,256]{1,0:T(8,128)S(1)}, f32[8,256]{1,0:T(8,128)S(1)}, u32[]{:S(2)}, u32[]{:S(2)}) %collective-permute-start.24) | collective-permute-done | bytes 8224 | tf_op jit(solution)/shard_map/ppermute | solution.py:27
  95.2 3.2 %collective-permute-done.25 = f32[8,256]{1,0:T(8,128)S(1)} collective-permute-done((f32[8,256]{1,0:T(8,128)S(1)}, f32[8,256]{1,0:T(8,128)S(1)}, u32[]{:S(2)}, u32[]{:S(2)}) %collective-permute-start.25) | collective-permute-done | bytes 8224 | tf_op jit(solution)/shard_map/ppermute | solution.py:27
  98.5 0.7 add_reduce_fusion
  99.2 0.3 fusion.5
  99.5 0.3 convolution_convert_fusion.2.grad_ref
  99.8 5.1 %shard_map.85 = (f32[128,4096]{1,0:T(8,128)S(1)}, f32[128,4096]{1,0:T(8,128)}) custom-call(bf16[256,512]{1,0:T(8,128)(2,1)S(1)} %convolution_convert_fusion.2.grad_ref, bf16[4096,512]{1,0:T(8,128)(2,1)} %head_ref.7), custom_call_target="tpu_custom_call" | custom-call | flops 4000000000 | bytes 10000000 | tf_op jit(solution)/shard_map/pallas_call | solution.py:283
  104.9 0.2 multiply_convert_fusion.1
  105.2 2.6 %collective-permute-done.26 = f16[128,4096]{1,0:T(8,128)(2,1)S(1)} collective-permute-done((f16[128,4096]{1,0:T(8,128)(2,1)S(1)}, f16[128,4096]{1,0:T(8,128)(2,1)S(1)}, u32[]{:S(2)}, u32[]{:S(2)}) %collective-permute-start.26) | collective-permute-done | bytes 1048608 | tf_op jit(solution)/shard_map/ppermute | solution.py:22
  107.8 0.4 multiply_convert_fusion
  108.3 0.1 fusion.54
  108.5 2.6 %collective-permute-start.28 = (f16[32,4096]{1,0:T(8,128)(2,1)S(1)}, f16[32,4096]{1,0:T(8,128)(2,1)S(1)}, u32[]{:S(2)}, u32[]{:S(2)}) collective-permute-start(f16[32,4096]{1,0:T(8,128)(2,1)S(1)} %get-tuple-element.68), channel_id=1, source_target_pairs={{0,32},{16,48},{32,0},{48,16},{1,33},{17,49},{33,1},{49,17},{2,34}... | collective-permute-start | bytes 786440 | tf_op jit(solution)/shard_map/ppermute | solution.py:22
  111.1 0.6 collective-permute-start.29
  111.7 11.9 %collective-permute-done.27 = f16[32,4096]{1,0:T(8,128)(2,1)S(1)} collective-permute-done((f16[32,4096]{1,0:T(8,128)(2,1)S(1)}, f16[32,4096]{1,0:T(8,128)(2,1)S(1)}, u32[]{:S(2)}, u32[]{:S(2)}) %collective-permute-start.27) | collective-permute-done | bytes 262176 | tf_op jit(solution)/shard_map/ppermute | solution.py:22
  123.7 0.6 collective-permute-done.29
  124.3 0.2 multiply_convert_fusion.2
  124.6 3.8 %collective-permute-start.31 = (f16[8,4096]{1,0:T(8,128)(2,1)S(1)}, f16[8,4096]{1,0:T(8,128)(2,1)S(1)}, u32[]{:S(2)}, u32[]{:S(2)}) collective-permute-start(f16[8,4096]{1,0:T(8,128)(2,1)S(1)} %get-tuple-element.71), channel_id=1, source_target_pairs={{0,4},{2,6},{4,0},{6,2},{1,5},{3,7},{5,1},{7,3},{8,12},{10,14},{12... | collective-permute-start | bytes 196616 | tf_op jit(solution)/shard_map/ppermute | solution.py:22
  128.4 1.7 %collective-permute-done.30 = f16[8,4096]{1,0:T(8,128)(2,1)S(1)} collective-permute-done((f16[8,4096]{1,0:T(8,128)(2,1)S(1)}, f16[8,4096]{1,0:T(8,128)(2,1)S(1)}, u32[]{:S(2)}, u32[]{:S(2)}) %collective-permute-start.30) | collective-permute-done | bytes 65568 | tf_op jit(solution)/shard_map/ppermute | solution.py:22
  130.1 1.2 collective-permute-done.31
  131.4 1.3 collective-permute-done.32
  132.9 1.5 %collective-permute-start.34 = (f32[2,4096]{1,0:T(2,128)S(1)}, f32[2,4096]{1,0:T(2,128)S(1)}, u32[]{:S(2)}, u32[]{:S(2)}) collective-permute-start(f32[2,4096]{1,0:T(2,128)S(1)} %get-tuple-element.72), channel_id=1, source_target_pairs={{0,8},{8,0},{64,72},{72,64},{1,9},{9,1},{65,73},{73,65},{2,10},{10... | collective-permute-start | bytes 98312 | tf_op jit(solution)/shard_map/ppermute | solution.py:27
  134.3 3.2 %collective-permute-start.35 = (f32[2,4096]{1,0:T(2,128)S(1)}, f32[2,4096]{1,0:T(2,128)S(1)}, u32[]{:S(2)}, u32[]{:S(2)}) collective-permute-start(f32[2,4096]{1,0:T(2,128)S(1)} %get-tuple-element.73), channel_id=1, source_target_pairs={{0,72},{8,64},{64,8},{72,0},{1,73},{9,65},{65,9},{73,1},{2,74},{10... | collective-permute-start | bytes 98312 | tf_op jit(solution)/shard_map/ppermute | solution.py:27
  137.6 3.3 %convolution_convert_fusion = bf16[4096,512]{1,0:T(8,128)(2,1)} fusion(bf16[256,4096]{1,0:T(8,128)(2,1)S(1)} %copy-done.5, bf16[256,512]{1,0:T(8,128)(2,1)S(1)} %fusion.5), kind=kOutput, calls=%fused_computation | convolution fusion | flops 1075838976 | bytes 6553600 | tf_op jit(solution)/shard_map/dot_general | solution.py:375
  141.6 0.6 slice_add_fusion.2
  (82 shorter events, 1.7 us)
Async XLA Ops:
  0.6 13.6 %collective-permute-start.1 = (bf16[2,4096]{1,0:T(2,128)(2,1)}, bf16[2,4096]{1,0:T(2,128)(2,1)S(1)}, u32[]{:S(2)}, u32[]{:S(2)}) collective-permute-start(bf16[2,4096]{1,0:T(2,128)(2,1)} %r0.1), channel_id=1, source_target_pairs={{0,64},{8,72},{64,0},{72,8},{1,65},{9,73},{65,1},{73,9},{2,66},{10... | collective-permute-start | bytes 49160 | tf_op jit(solution)/shard_map/ppermute | solution.py:27
  2.7 11.6 %collective-permute-start.2 = (bf16[2,4096]{1,0:T(2,128)(2,1)}, bf16[2,4096]{1,0:T(2,128)(2,1)S(1)}, u32[]{:S(2)}, u32[]{:S(2)}) collective-permute-start(bf16[2,4096]{1,0:T(2,128)(2,1)} %r0.1), channel_id=1, source_target_pairs={{0,8},{8,0},{64,72},{72,64},{1,9},{9,1},{65,73},{73,65},{2,10},{10... | collective-permute-start | bytes 49160 | tf_op jit(solution)/shard_map/ppermute | solution.py:27
  6.3 8.0 %collective-permute-start.3 = (bf16[2,4096]{1,0:T(2,128)(2,1)}, bf16[2,4096]{1,0:T(2,128)(2,1)S(1)}, u32[]{:S(2)}, u32[]{:S(2)}) collective-permute-start(bf16[2,4096]{1,0:T(2,128)(2,1)} %r0.1), channel_id=1, source_target_pairs={{0,72},{8,64},{64,8},{72,0},{1,73},{9,65},{65,9},{73,1},{2,74},{10... | collective-permute-start | bytes 49160 | tf_op jit(solution)/shard_map/ppermute | solution.py:27
  6.3 1.0 copy-start.1
  7.4 6.9 %copy-start.3 = (bf16[2,4096]{1,0:T(2,128)(2,1)S(1)}, bf16[2,4096]{1,0:T(2,128)(2,1)}, u32[]{:S(2)}) copy-start(bf16[2,4096]{1,0:T(2,128)(2,1)} %r0.1) | copy-start | bytes 49156
  14.1 4.9 %copy-start.2 = (bf16[256,1024]{1,0:T(8,128)(2,1)S(1)}, bf16[256,1024]{1,0:T(8,128)(2,1)}, u32[]{:S(2)}) copy-start(bf16[256,1024]{1,0:T(8,128)(2,1)} %hidden_ref.5) | copy-start | bytes 1572868
  14.1 12.1 %collective-permute-start = (s16[8,256,640]{2,1,0:T(8,128)(2,1)S(1)}, s16[8,256,640]{2,1,0:T(8,128)(2,1)S(1)}, u32[]{:S(2)}, u32[]{:S(2)}) collective-permute-start(s16[8,256,640]{2,1,0:T(8,128)(2,1)S(1)} %shard_map.77), channel_id=1, source_target_pairs={{0,1},{1,0},{2,3},{3,2},{4,5},{5,4},{6,7},{7,6},{8,9},{9,8},{10,11... | collective-permute-start | bytes 7864328 | tf_op jit(solution)/shard_map/ppermute | solution.py:22
  14.3 8.3 %collective-permute-start.4 = (bf16[8,4096]{1,0:T(8,128)(2,1)S(1)}, bf16[8,4096]{1,0:T(8,128)(2,1)S(1)}, u32[]{:S(2)}, u32[]{:S(2)}) collective-permute-start(bf16[8,4096]{1,0:T(8,128)(2,1)S(1)} %shard_map.78.refs_0_), channel_id=1, source_target_pairs={{2,0},{4,2},{6,4},{0,6},{3,1},{5,3},{7,5},{1,7},{10,8},{12,10},{14... | collective-permute-start | bytes 196616 | tf_op jit(solution)/shard_map/ppermute | solution.py:17
  17.4 6.4 %collective-permute-start.5 = (bf16[8,4096]{1,0:T(8,128)(2,1)S(1)}, bf16[8,4096]{1,0:T(8,128)(2,1)S(1)}, u32[]{:S(2)}, u32[]{:S(2)}) collective-permute-start(bf16[8,4096]{1,0:T(8,128)(2,1)S(1)} %shard_map.78.refs_0_), channel_id=1, source_target_pairs={{4,0},{6,2},{0,4},{2,6},{5,1},{7,3},{1,5},{3,7},{12,8},{14,10},{8,... | collective-permute-start | bytes 196616 | tf_op jit(solution)/shard_map/ppermute | solution.py:17
  18.0 6.5 %collective-permute-start.6 = (bf16[8,4096]{1,0:T(8,128)(2,1)S(1)}, bf16[8,4096]{1,0:T(8,128)(2,1)S(1)}, u32[]{:S(2)}, u32[]{:S(2)}) collective-permute-start(bf16[8,4096]{1,0:T(8,128)(2,1)S(1)} %shard_map.78.refs_0_), channel_id=1, source_target_pairs={{6,0},{0,2},{2,4},{4,6},{7,1},{1,3},{3,5},{5,7},{14,8},{8,10},{10,... | collective-permute-start | bytes 196616 | tf_op jit(solution)/shard_map/ppermute | solution.py:17
  22.6 2.0 %copy-start = (f32[4,256,512]{2,1,0:T(8,128)}, f32[4,256,512]{2,1,0:T(8,128)S(1)}, u32[]{:S(2)}) copy-start(f32[4,256,512]{2,1,0:T(8,128)S(1)} %shard_map.76.first_ref) | copy-start | bytes 6291460
  24.6 11.2 %collective-permute-start.15 = (bf16[32,4096]{1,0:T(8,128)(2,1)S(1)}, bf16[32,4096]{1,0:T(8,128)(2,1)S(1)}, u32[]{:S(2)}, u32[]{:S(2)}) collective-permute-start(bf16[32,4096]{1,0:T(8,128)(2,1)S(1)} %shard_map.79.refs_0_), channel_id=1, source_target_pairs={{0,16},{16,0},{32,48},{48,32},{1,17},{17,1},{33,49},{49,33},{2,18}... | collective-permute-start | bytes 786440 | tf_op jit(solution)/shard_map/ppermute | solution.py:319
  26.1 1.5 %copy-start.9 = (s16[8,256,640]{2,1,0:T(8,128)(2,1)}, s16[8,256,640]{2,1,0:T(8,128)(2,1)S(1)}, u32[]{:S(2)}) copy-start(s16[8,256,640]{2,1,0:T(8,128)(2,1)S(1)} %collective-permute-done.other_ref) | copy-start | bytes 7864324
  33.8 20.3 %collective-permute-start.10 = (s16[128,2176]{1,0:T(8,128)(2,1)S(1)}, s16[128,2176]{1,0:T(8,128)(2,1)S(1)}, u32[]{:S(2)}, u32[]{:S(2)}) collective-permute-start(s16[128,2176]{1,0:T(8,128)(2,1)S(1)} %get-tuple-element.24), channel_id=1, source_target_pairs={{0,8},{8,0},{1,9},{9,1},{2,10},{10,2},{3,11},{11,3},{4,12},{12,4},... | collective-permute-start | bytes 1671176 | tf_op jit(solution)/shard_map/ppermute | solution.py:22
  35.8 19.0 %collective-permute-start.16 = (bf16[64,4096]{1,0:T(8,128)(2,1)S(1)}, bf16[64,4096]{1,0:T(8,128)(2,1)S(1)}, u32[]{:S(2)}, u32[]{:S(2)}) collective-permute-start(bf16[64,4096]{1,0:T(8,128)(2,1)S(1)} %shard_map.82.refs_0_), channel_id=1, source_target_pairs={{0,48},{48,0},{16,32},{32,16},{1,49},{49,1},{17,33},{33,17},{2,50}... | collective-permute-start | bytes 1572872 | tf_op jit(solution)/shard_map/ppermute | solution.py:328
  38.0 15.5 %collective-permute-start.7 = (s16[128,1152]{1,0:T(8,128)(2,1)S(1)}, s16[128,1152]{1,0:T(8,128)(2,1)S(1)}, u32[]{:S(2)}, u32[]{:S(2)}) collective-permute-start(s16[128,1152]{1,0:T(8,128)(2,1)S(1)} %get-tuple-element.20), channel_id=1, source_target_pairs={{0,2},{2,4},{4,6},{6,0},{1,3},{3,5},{5,7},{7,1},{8,10},{10,12},{12... | collective-permute-start | bytes 884744 | tf_op jit(solution)/shard_map/ppermute | solution.py:22
  39.1 14.3 %collective-permute-start.8 = (s16[128,1152]{1,0:T(8,128)(2,1)S(1)}, s16[128,1152]{1,0:T(8,128)(2,1)S(1)}, u32[]{:S(2)}, u32[]{:S(2)}) collective-permute-start(s16[128,1152]{1,0:T(8,128)(2,1)S(1)} %get-tuple-element.21), channel_id=1, source_target_pairs={{0,4},{2,6},{4,0},{6,2},{1,5},{3,7},{5,1},{7,3},{8,12},{10,14},{12... | collective-permute-start | bytes 884744 | tf_op jit(solution)/shard_map/ppermute | solution.py:22
  41.0 13.1 %collective-permute-start.9 = (s16[128,1152]{1,0:T(8,128)(2,1)S(1)}, s16[128,1152]{1,0:T(8,128)(2,1)S(1)}, u32[]{:S(2)}, u32[]{:S(2)}) collective-permute-start(s16[128,1152]{1,0:T(8,128)(2,1)S(1)} %get-tuple-element.22), channel_id=1, source_target_pairs={{0,6},{2,0},{4,2},{6,4},{1,7},{3,1},{5,3},{7,5},{8,14},{10,8},{12,... | collective-permute-start | bytes 884744 | tf_op jit(solution)/shard_map/ppermute | solution.py:22
  54.9 6.2 %collective-permute-start.17 = (bf16[128,4096]{1,0:T(8,128)(2,1)S(1)}, bf16[128,4096]{1,0:T(8,128)(2,1)S(1)}, u32[]{:S(2)}, u32[]{:S(2)}) collective-permute-start(bf16[128,4096]{1,0:T(8,128)(2,1)S(1)} %shard_map.83), channel_id=1, source_target_pairs={{1,0},{0,1},{3,2},{2,3},{5,4},{4,5},{7,6},{6,7},{9,8},{8,9},{11,10... | collective-permute-start | bytes 3145736 | tf_op jit(solution)/shard_map/ppermute | solution.py:17
  55.1 9.6 %collective-permute-start.11 = (s16[128,640]{1,0:T(8,128)(2,1)S(1)}, s16[128,640]{1,0:T(8,128)(2,1)S(1)}, u32[]{:S(2)}, u32[]{:S(2)}) collective-permute-start(s16[128,640]{1,0:T(8,128)(2,1)S(1)} %get-tuple-element.26), channel_id=1, source_target_pairs={{0,8},{8,0},{1,9},{9,1},{2,10},{10,2},{3,11},{11,3},{4,12},{12,4},... | collective-permute-start | bytes 491528 | tf_op jit(solution)/shard_map/ppermute | solution.py:22
  57.0 7.7 %collective-permute-start.12 = (s16[128,640]{1,0:T(8,128)(2,1)S(1)}, s16[128,640]{1,0:T(8,128)(2,1)S(1)}, u32[]{:S(2)}, u32[]{:S(2)}) collective-permute-start(s16[128,640]{1,0:T(8,128)(2,1)S(1)} %get-tuple-element.28), channel_id=1, source_target_pairs={{0,2},{2,4},{4,6},{6,0},{1,3},{3,5},{5,7},{7,1},{8,10},{10,12},{12... | collective-permute-start | bytes 491528 | tf_op jit(solution)/shard_map/ppermute | solution.py:22
  57.6 11.3 %collective-permute-start.13 = (s16[128,640]{1,0:T(8,128)(2,1)S(1)}, s16[128,640]{1,0:T(8,128)(2,1)S(1)}, u32[]{:S(2)}, u32[]{:S(2)}) collective-permute-start(s16[128,640]{1,0:T(8,128)(2,1)S(1)} %get-tuple-element.29), channel_id=1, source_target_pairs={{0,4},{2,6},{4,0},{6,2},{1,5},{3,7},{5,1},{7,3},{8,12},{10,14},{12... | collective-permute-start | bytes 491528 | tf_op jit(solution)/shard_map/ppermute | solution.py:22
  61.1 2.2 %copy-start.8 = (bf16[4096,512]{1,0:T(8,128)(2,1)S(1)}, bf16[4096,512]{1,0:T(8,128)(2,1)}, u32[]{:S(2)}) copy-start(bf16[4096,512]{1,0:T(8,128)(2,1)} %head_ref.7) | copy-start | bytes 12582916
  61.1 7.8 %collective-permute-start.14 = (s16[128,640]{1,0:T(8,128)(2,1)S(1)}, s16[128,640]{1,0:T(8,128)(2,1)S(1)}, u32[]{:S(2)}, u32[]{:S(2)}) collective-permute-start(s16[128,640]{1,0:T(8,128)(2,1)S(1)} %get-tuple-element.30), channel_id=1, source_target_pairs={{0,6},{2,0},{4,2},{6,4},{1,7},{3,1},{5,3},{7,5},{8,14},{10,8},{12,... | collective-permute-start | bytes 491528 | tf_op jit(solution)/shard_map/ppermute | solution.py:22
  63.3 1.4 copy-start.4
  64.7 4.6 %copy-start.7 = (s32[256]{0:T(256)S(1)}, s32[256]{0:T(256)}, u32[]{:S(2)}) copy-start(s32[256]{0:T(256)} %param.9) | copy-start | bytes 3076
  69.8 1.2 collective-permute-start.18
  71.1 3.7 %collective-permute-start.19 = (f32[8,256]{1,0:T(8,128)S(1)}, f32[8,256]{1,0:T(8,128)S(1)}, u32[]{:S(2)}, u32[]{:S(2)}) collective-permute-start(f32[8,256]{1,0:T(8,128)S(1)} %stack.34), channel_id=1, source_target_pairs={{0,16},{16,0},{32,48},{48,32},{1,17},{17,1},{33,49},{49,33},{2,18}... | collective-permute-start | bytes 24584 | tf_op jit(solution)/shard_map/ppermute | solution.py:57
  74.9 4.9 %collective-permute-start.20 = (f32[8,256]{1,0:T(8,128)S(1)}, f32[8,256]{1,0:T(8,128)S(1)}, u32[]{:S(2)}, u32[]{:S(2)}) collective-permute-start(f32[8,256]{1,0:T(8,128)S(1)} %stack.35), channel_id=1, source_target_pairs={{0,48},{48,0},{16,32},{32,16},{1,49},{49,1},{17,33},{33,17},{2,50}... | collective-permute-start | bytes 24584 | tf_op jit(solution)/shard_map/ppermute | solution.py:57
  79.9 3.7 %collective-permute-start.21 = (f32[8,256]{1,0:T(8,128)S(1)}, f32[8,256]{1,0:T(8,128)S(1)}, u32[]{:S(2)}, u32[]{:S(2)}) collective-permute-start(f32[8,256]{1,0:T(8,128)S(1)} %stack.36), channel_id=1, source_target_pairs={{0,2},{2,0},{4,6},{6,4},{1,3},{3,1},{5,7},{7,5},{8,10},{10,8},{12,... | collective-permute-start | bytes 24584 | tf_op jit(solution)/shard_map/ppermute | solution.py:57
  83.7 4.9 %collective-permute-start.22 = (f32[8,256]{1,0:T(8,128)S(1)}, f32[8,256]{1,0:T(8,128)S(1)}, u32[]{:S(2)}, u32[]{:S(2)}) collective-permute-start(f32[8,256]{1,0:T(8,128)S(1)} %stack.37), channel_id=1, source_target_pairs={{0,6},{6,0},{2,4},{4,2},{1,7},{7,1},{3,5},{5,3},{8,14},{14,8},{10,... | collective-permute-start | bytes 24584 | tf_op jit(solution)/shard_map/ppermute | solution.py:57
  88.7 4.9 %collective-permute-start.23 = (f32[8,256]{1,0:T(8,128)S(1)}, f32[8,256]{1,0:T(8,128)S(1)}, u32[]{:S(2)}, u32[]{:S(2)}) collective-permute-start(f32[8,256]{1,0:T(8,128)S(1)} %stack.38), channel_id=1, source_target_pairs={{0,64},{8,72},{64,0},{72,8},{1,65},{9,73},{65,1},{73,9},{2,66},{10... | collective-permute-start | bytes 24584 | tf_op jit(solution)/shard_map/ppermute | solution.py:27
  89.8 5.5 %collective-permute-start.24 = (f32[8,256]{1,0:T(8,128)S(1)}, f32[8,256]{1,0:T(8,128)S(1)}, u32[]{:S(2)}, u32[]{:S(2)}) collective-permute-start(f32[8,256]{1,0:T(8,128)S(1)} %stack.38), channel_id=1, source_target_pairs={{0,8},{8,0},{64,72},{72,64},{1,9},{9,1},{65,73},{73,65},{2,10},{10... | collective-permute-start | bytes 24584 | tf_op jit(solution)/shard_map/ppermute | solution.py:27
  93.6 4.9 %collective-permute-start.25 = (f32[8,256]{1,0:T(8,128)S(1)}, f32[8,256]{1,0:T(8,128)S(1)}, u32[]{:S(2)}, u32[]{:S(2)}) collective-permute-start(f32[8,256]{1,0:T(8,128)S(1)} %stack.38), channel_id=1, source_target_pairs={{0,72},{8,64},{64,8},{72,0},{1,73},{9,65},{65,9},{73,1},{2,74},{10... | collective-permute-start | bytes 24584 | tf_op jit(solution)/shard_map/ppermute | solution.py:27
  104.9 3.0 %copy-start.6 = (f32[128,4096]{1,0:T(8,128)S(1)}, f32[128,4096]{1,0:T(8,128)}, u32[]{:S(2)}) copy-start(f32[128,4096]{1,0:T(8,128)} %get-tuple-element.33) | copy-start | bytes 6291460
  105.1 2.7 %collective-permute-start.26 = (f16[128,4096]{1,0:T(8,128)(2,1)S(1)}, f16[128,4096]{1,0:T(8,128)(2,1)S(1)}, u32[]{:S(2)}, u32[]{:S(2)}) collective-permute-start(f16[128,4096]{1,0:T(8,128)(2,1)S(1)} %multiply_convert_fusion.1), channel_id=1, source_target_pairs={{0,1},{1,0},{2,3},{3,2},{4,5},{5,4},{6,7},{7,6},{8,9},{9,8},{10,11... | collective-permute-start | bytes 3145736 | tf_op jit(solution)/shard_map/ppermute | solution.py:22
  108.2 29.3 %copy-start.5 = (bf16[256,4096]{1,0:T(8,128)(2,1)S(1)}, bf16[256,4096]{1,0:T(8,128)(2,1)}, u32[]{:S(2)}) copy-start(bf16[256,4096]{1,0:T(8,128)(2,1)} %copy-done.4) | copy-start | bytes 6291460
  108.4 15.2 %collective-permute-start.27 = (f16[32,4096]{1,0:T(8,128)(2,1)S(1)}, f16[32,4096]{1,0:T(8,128)(2,1)S(1)}, u32[]{:S(2)}, u32[]{:S(2)}) collective-permute-start(f16[32,4096]{1,0:T(8,128)(2,1)S(1)} %get-tuple-element.66), channel_id=1, source_target_pairs={{0,16},{16,32},{32,48},{48,0},{1,17},{17,33},{33,49},{49,1},{2,18}... | collective-permute-start | bytes 786440 | tf_op jit(solution)/shard_map/ppermute | solution.py:22
  108.5 15.2 %collective-permute-start.28 = (f16[32,4096]{1,0:T(8,128)(2,1)S(1)}, f16[32,4096]{1,0:T(8,128)(2,1)S(1)}, u32[]{:S(2)}, u32[]{:S(2)}) collective-permute-start(f16[32,4096]{1,0:T(8,128)(2,1)S(1)} %get-tuple-element.68), channel_id=1, source_target_pairs={{0,32},{16,48},{32,0},{48,16},{1,33},{17,49},{33,1},{49,17},{2,34}... | collective-permute-start | bytes 786440 | tf_op jit(solution)/shard_map/ppermute | solution.py:22
  111.1 13.2 %collective-permute-start.29 = (f16[32,4096]{1,0:T(8,128)(2,1)S(1)}, f16[32,4096]{1,0:T(8,128)(2,1)S(1)}, u32[]{:S(2)}, u32[]{:S(2)}) collective-permute-start(f16[32,4096]{1,0:T(8,128)(2,1)S(1)} %get-tuple-element.67), channel_id=1, source_target_pairs={{0,48},{16,0},{32,16},{48,32},{1,49},{17,1},{33,17},{49,33},{2,50}... | collective-permute-start | bytes 786440 | tf_op jit(solution)/shard_map/ppermute | solution.py:22
  124.5 5.6 %collective-permute-start.30 = (f16[8,4096]{1,0:T(8,128)(2,1)S(1)}, f16[8,4096]{1,0:T(8,128)(2,1)S(1)}, u32[]{:S(2)}, u32[]{:S(2)}) collective-permute-start(f16[8,4096]{1,0:T(8,128)(2,1)S(1)} %get-tuple-element.69), channel_id=1, source_target_pairs={{0,2},{2,4},{4,6},{6,0},{1,3},{3,5},{5,7},{7,1},{8,10},{10,12},{12... | collective-permute-start | bytes 196616 | tf_op jit(solution)/shard_map/ppermute | solution.py:22
  124.6 6.8 %collective-permute-start.31 = (f16[8,4096]{1,0:T(8,128)(2,1)S(1)}, f16[8,4096]{1,0:T(8,128)(2,1)S(1)}, u32[]{:S(2)}, u32[]{:S(2)}) collective-permute-start(f16[8,4096]{1,0:T(8,128)(2,1)S(1)} %get-tuple-element.71), channel_id=1, source_target_pairs={{0,4},{2,6},{4,0},{6,2},{1,5},{3,7},{5,1},{7,3},{8,12},{10,14},{12... | collective-permute-start | bytes 196616 | tf_op jit(solution)/shard_map/ppermute | solution.py:22
  128.4 4.3 %collective-permute-start.32 = (f16[8,4096]{1,0:T(8,128)(2,1)S(1)}, f16[8,4096]{1,0:T(8,128)(2,1)S(1)}, u32[]{:S(2)}, u32[]{:S(2)}) collective-permute-start(f16[8,4096]{1,0:T(8,128)(2,1)S(1)} %get-tuple-element.70), channel_id=1, source_target_pairs={{0,6},{2,0},{4,2},{6,4},{1,7},{3,1},{5,3},{7,5},{8,14},{10,8},{12,... | collective-permute-start | bytes 196616 | tf_op jit(solution)/shard_map/ppermute | solution.py:22
  132.8 8.8 %collective-permute-start.33 = (f32[2,4096]{1,0:T(2,128)S(1)}, f32[2,4096]{1,0:T(2,128)S(1)}, u32[]{:S(2)}, u32[]{:S(2)}) collective-permute-start(f32[2,4096]{1,0:T(2,128)S(1)} %get-tuple-element.74), channel_id=1, source_target_pairs={{0,64},{8,72},{64,0},{72,8},{1,65},{9,73},{65,1},{73,9},{2,66},{10... | collective-permute-start | bytes 98312 | tf_op jit(solution)/shard_map/ppermute | solution.py:27
  132.9 8.7 %collective-permute-start.34 = (f32[2,4096]{1,0:T(2,128)S(1)}, f32[2,4096]{1,0:T(2,128)S(1)}, u32[]{:S(2)}, u32[]{:S(2)}) collective-permute-start(f32[2,4096]{1,0:T(2,128)S(1)} %get-tuple-element.72), channel_id=1, source_target_pairs={{0,8},{8,0},{64,72},{72,64},{1,9},{9,1},{65,73},{73,65},{2,10},{10... | collective-permute-start | bytes 98312 | tf_op jit(solution)/shard_map/ppermute | solution.py:27
  134.3 7.2 %collective-permute-start.35 = (f32[2,4096]{1,0:T(2,128)S(1)}, f32[2,4096]{1,0:T(2,128)S(1)}, u32[]{:S(2)}, u32[]{:S(2)}) collective-permute-start(f32[2,4096]{1,0:T(2,128)S(1)} %get-tuple-element.73), channel_id=1, source_target_pairs={{0,72},{8,64},{64,8},{72,0},{1,73},{9,65},{65,9},{73,1},{2,74},{10... | collective-permute-start | bytes 98312 | tf_op jit(solution)/shard_map/ppermute | solution.py:27

commit v2 on v1

--- a/solution.py
+++ b/solution.py
@@ -82,6 +82,28 @@
     ref[:, n : n + 128] = jnp.broadcast_to(code, (code.shape[0], 128)).astype(i16)
 
 
+def pack(ref, blocks, code):
+    inverse = 1.0 / step_of(code)
+    for i, block in enumerate(blocks):
+        whole = jnp.round(block * inverse).astype(i16)
+        for g in range(4):
+            at = (4 * i + g) * 128
+            ref[at : at + 128] = whole[:, g * 128 : (g + 1) * 128]
+    codes = jnp.transpose(jnp.broadcast_to(code, (128, 128)))
+    ref[len(blocks) * 512 :] = codes[:16].astype(i16)
+
+
+def unpack(ref):
+    count = ref.shape[0] // 512
+    codes = ref[count * 512 :].astype(f32)[:1]
+    step = step_of(jnp.transpose(jnp.broadcast_to(codes, (128, 128)))[:, :1])
+    blocks = []
+    for i in range(count):
+        tiles = [ref[(4 * i + g) * 128 : (4 * i + g + 1) * 128].astype(f32) * step for g in range(4)]
+        blocks.append(jnp.concatenate(tiles, axis=1))
+    return blocks
+
+
 def take(ref, i, count):
     step = step_of(ref[:, count * 512 : count * 512 + 128].astype(f32)[:, :1])
     return ref[:, i * 512 : (i + 1) * 512].astype(f32) * step
@@ -96,12 +118,16 @@
 in_smem = pl.BlockSpec(memory_space=pltpu.SMEM)
 
 
-def fetch_blocks(order_ref, head_ref, held, sems):
+def fetch_blocks(order_ref, hidden_ref, head_ref, rows, held, sems):
+    count = held.shape[0]
     copies = []
-    for j in range(held.shape[0]):
+    whole = pltpu.make_async_copy(hidden_ref, rows, sems.at[count])
+    whole.start()
+    for j in range(count):
         columns = pl.ds(pl.multiple_of(order_ref[j] * 512, 512), 512)
         copies.append(pltpu.make_async_copy(head_ref.at[:, columns], held.at[j], sems.at[j]))
         copies[-1].start()
+    whole.wait()
     return copies
 
 
@@ -109,19 +135,23 @@
     count = order.shape[0]
     rows, depth = hidden.shape
 
-    def kernel(order_ref, hidden_ref, head_ref, out_ref, held, sems):
-        copies = fetch_blocks(order_ref, head_ref, held, sems)
+    def kernel(order_ref, hidden_ref, head_ref, out_ref, rows_ref, held, sems):
+        copies = fetch_blocks(order_ref, hidden_ref, head_ref, rows_ref, held, sems)
         for j in range(count):
             copies[j].wait()
-            block = jnp.dot(hidden_ref[...], held[j], preferred_element_type=f32)
+            block = jnp.dot(rows_ref[...], held[j], preferred_element_type=f32)
             put(out_ref.at[j], [block], row_code(top_of([block])))
 
     return pl.pallas_call(
         kernel,
-        in_specs=[in_smem, in_vmem, anywhere],
+        in_specs=[in_smem, anywhere, anywhere],
         out_specs=in_vmem,
         out_shape=jax.ShapeDtypeStruct((count, rows, 640), i16),
-        scratch_shapes=[pltpu.VMEM((count, depth, 512), bf16), pltpu.SemaphoreType.DMA((count,))],
+        scratch_shapes=[
+            pltpu.VMEM((rows, depth), bf16),
+            pltpu.VMEM((count, depth, 512), bf16),
+            pltpu.SemaphoreType.DMA((count + 1,)),
+        ],
         compiler_params=pltpu.CompilerParams(vmem_limit_bytes=50 << 20),
         cost_estimate=cost(6),
     )(order, hidden, head)
@@ -131,18 +161,22 @@
     count = order.shape[0]
     rows, depth = hidden.shape
 
-    def kernel(order_ref, hidden_ref, head_ref, out_ref, held, sems):
-        copies = fetch_blocks(order_ref, head_ref, held, sems)
+    def kernel(order_ref, hidden_ref, head_ref, out_ref, rows_ref, held, sems):
+        copies = fetch_blocks(order_ref, hidden_ref, head_ref, rows_ref, held, sems)
         for j in range(count):
             copies[j].wait()
-            out_ref[j] = jnp.dot(hidden_ref[...], held[j], preferred_element_type=f32)
+            out_ref[j] = jnp.dot(rows_ref[...], held[j], preferred_element_type=f32)
 
     return pl.pallas_call(
         kernel,
-        in_specs=[in_smem, in_vmem, anywhere],
+        in_specs=[in_smem, anywhere, anywhere],
         out_specs=in_vmem,
         out_shape=jax.ShapeDtypeStruct((count, rows, 512), f32),
-        scratch_shapes=[pltpu.VMEM((count, depth, 512), bf16), pltpu.SemaphoreType.DMA((count,))],
+        scratch_shapes=[
+            pltpu.VMEM((rows, depth), bf16),
+            pltpu.VMEM((count, depth, 512), bf16),
+            pltpu.SemaphoreType.DMA((count + 1,)),
+        ],
         compiler_params=pltpu.CompilerParams(vmem_limit_bytes=50 << 20),
         cost_estimate=cost(4),
     )(order, hidden, head)
@@ -153,15 +187,15 @@
     half = rows // 2
 
     def kernel(order_ref, hidden_ref, head_ref, first_ref, other_ref, *refs):
-        a1, a2, a3, b1, keep_a, keep_b, held, sums, sems = refs[len(ready) :]
-        copies = fetch_blocks(order_ref, head_ref, held, sems)
+        a1, a2, a3, b1, keep_a, keep_b, rows_ref, held, sums, sems = refs[len(ready) :]
+        copies = fetch_blocks(order_ref, hidden_ref, head_ref, rows_ref, held, sems)
         up, low = jnp.zeros((half, 1), f32), jnp.zeros((half, 1), f32)
         for j in range(8):
             if j < 4:
                 block = first_ref[j]
             else:
                 copies[j - 4].wait()
-                block = jnp.dot(hidden_ref[...], held[j - 4], preferred_element_type=f32)
+                block = jnp.dot(rows_ref[...], held[j - 4], preferred_element_type=f32)
             block += take(other_ref.at[j], 0, 1)
             top = jnp.max(jnp.abs(block), axis=1, keepdims=True)
             if j % 4:
@@ -176,21 +210,22 @@
                 keep_b[:, j * 512 : j * 512 + 512] = block[half:]
         code = row_code(up)
         for d, ref in ((1, a1), (2, a2), (3, a3)):
-            put(ref, [sums[d, :half], sums[4 + d, :half]], code)
-        put(b1, [sums[4 + d, half:] for d in range(4)], row_code(low))
-
-    outs = [(half, 1152, i16)] * 3 + [(half, 2176, i16), (half, 1024, f32), (half, 2048, f32)]
+            pack(ref, [sums[d, :half], sums[4 + d, :half]], code)
+        pack(b1, [sums[4 + d, half:] for d in range(4)], row_code(low))
+
+    outs = [(1040, 128, i16)] * 3 + [(2064, 128, i16), (half, 1024, f32), (half, 2048, f32)]
     return pl.pallas_call(
         kernel,
-        in_specs=[in_smem, in_vmem, anywhere, in_vmem, in_vmem] + [anywhere] * len(ready),
+        in_specs=[in_smem, anywhere, anywhere, in_vmem, in_vmem] + [anywhere] * len(ready),
         out_specs=[in_vmem] * len(outs),
         out_shape=[jax.ShapeDtypeStruct((m, n), d) for m, n, d in outs],
         scratch_shapes=[
+            pltpu.VMEM((rows, depth), bf16),
             pltpu.VMEM((4, depth, 512), bf16),
             pltpu.VMEM((8, rows, 512), f32),
-            pltpu.SemaphoreType.DMA((4,)),
+            pltpu.SemaphoreType.DMA((5,)),
         ],
-        compiler_params=pltpu.CompilerParams(vmem_limit_bytes=50 << 20),
+        compiler_params=pltpu.CompilerParams(vmem_limit_bytes=44 << 20),
         cost_estimate=cost(7),
     )(order, hidden, head, first, other, *ready)
 
@@ -220,23 +255,27 @@
     out[...] = jnp.concatenate([r[...].astype(f32) for r in ins[:count]], axis=0).astype(bf16)
 
 
+def hand_on(value, *rest):
+    rest[-1][...] = value[...]
+
+
 def split_second(keep_a, r1, r2, r3, keep_b, rz, a1, b1, b2, b3, out_a, out_b):
+    got = [unpack(r) for r in (r1, r2, r3)]
     mine, other = [
-        keep_a[:, i * 512 : (i + 1) * 512] + take(r1, i, 2) + take(r2, i, 2) + take(r3, i, 2)
-        for i in range(2)
+        keep_a[:, i * 512 : (i + 1) * 512] + got[0][i] + got[1][i] + got[2][i] for i in range(2)
     ]
     out_a[...] = mine
-    put(a1, [other], row_code(top_of([other])))
-    low = [keep_b[:, d * 512 : (d + 1) * 512] + take(rz, d, 4) for d in range(4)]
+    pack(a1, [other], row_code(top_of([other])))
+    low = [keep_b[:, d * 512 : (d + 1) * 512] + g for d, g in enumerate(unpack(rz))]
     out_b[...] = low[0]
     code = row_code(top_of(low[1:]))
     for d, ref in ((1, b1), (2, b2), (3, b3)):
-        put(ref, [low[d]], code)
+        pack(ref, [low[d]], code)
 
 
 def join_last(keep_a, rz, keep_b, r1, r2, r3, _, out_a, out_b):
-    out_a[...] = keep_a[...] + take(rz, 0, 1)
-    out_b[...] = keep_b[...] + take(r1, 0, 1) + take(r2, 0, 1) + take(r3, 0, 1)
+    out_a[...] = keep_a[...] + unpack(rz)[0]
+    out_b[...] = keep_b[...] + unpack(r1)[0] + unpack(r2)[0] + unpack(r3)[0]
 
 
 def token_order(me):
@@ -261,44 +300,40 @@
     return (lax.broadcasted_iota(jnp.int32, (n, n), 0) == order[None, :]).astype(bf16)
 
 
-def grad_rows(grad, head):
+def grad_rows(grad, turn, head):
     feats, depth = head.shape
     steps = 8
     wide = feats // steps
 
-    def kernel(grad_ref, head_ref, far_ref, near_ref, held, sems):
-        copies = []
+    def kernel(grad_ref, turn_ref, head_ref, far_ref, near_ref):
+        rows = jnp.dot(turn_ref[...], grad_ref[...], preferred_element_type=f32).astype(bf16)
         for j in range(steps):
-            part = head_ref.at[pl.ds(j * wide, wide), :]
-            copies.append(pltpu.make_async_copy(part, held.at[j], sems.at[j]))
-            copies[-1].start()
-        for j in range(steps):
-            copies[j].wait()
+            at = slice(j * wide, (j + 1) * wide)
             both = lax.dot_general(
-                grad_ref[...], held[j], (((1,), (1,)), ((), ())), preferred_element_type=f32
+                rows, head_ref[at], (((1,), (1,)), ((), ())), preferred_element_type=f32
             )
-            near_ref[:, j * wide : (j + 1) * wide] = both[:128]
-            far_ref[:, j * wide : (j + 1) * wide] = both[128:]
+            near_ref[:, at] = both[:128]
+            far_ref[:, at] = both[128:]
 
     return pl.pallas_call(
         kernel,
-        in_specs=[in_vmem, anywhere],
+        in_specs=[in_vmem] * 3,
         out_specs=[in_vmem] * 2,
         out_shape=[jax.ShapeDtypeStruct((128, feats), f32)] * 2,
-        scratch_shapes=[pltpu.VMEM((steps, wide, depth), bf16), pltpu.SemaphoreType.DMA((steps,))],
-        compiler_params=pltpu.CompilerParams(vmem_limit_bytes=50 << 20),
-        cost_estimate=cost(4),
-    )(grad, head)
-
-
-def scatter_rows(far, near):
+        compiler_params=pltpu.CompilerParams(vmem_limit_bytes=24 << 20),
+        cost_estimate=cost(3),
+    )(grad, turn, head)
+
+
+def scatter_rows(far, near, ready):
     total = near + send((far * grad_scale).astype(f16), "c", 1).astype(f32) * (1.0 / grad_scale)
     out = (total * grad_scale).astype(f16).reshape(4, 32, -1)
-    got = [send(out[d], "x", d) for d in (1, 2, 3)]
+    got = [send(out[d], "x", d) for d in (2, 1, 3)]
     total = total[:32] + sum(g.astype(f32) for g in got) * (1.0 / grad_scale)
     out = (total * grad_scale).astype(f16).reshape(4, 8, -1)
-    got = [send(out[d], "y", d) for d in (1, 2, 3)]
-    total = total[:8] + sum(g.astype(f32) for g in got) * (1.0 / grad_scale)
+    got = [send(out[d], "y", d) for d in (2, 1, 3)]
+    (own,) = whole_call(hand_on, [total[:8]], [(8, total.shape[1], f32)], ready)
+    total = own + sum(g.astype(f32) for g in got) * (1.0 / grad_scale)
     across = ((1, ("zl",)), (2, ("zh",)), (3, ("zl", "zh")))
     return total[:2] + sum(cross_z(total[2 * i : 2 * i + 2], r) for i, r in across)
 
@@ -323,15 +358,15 @@
     a1, a2, a3, b1, keep_a, keep_b = own_products(
         teacher_hidden, teacher_head, column[4:] + c, first, other, [rows]
     )
-    a1, a2, a3, b1 = send(a1, "y", 1), send(a2, "y", 2), send(a3, "y", 3), send(b1, "zh", 1)
+    a2, b1, a1, a3 = send(a2, "y", 2), send(b1, "zh", 1), send(a1, "y", 1), send(a3, "y", 3)
     (rows,) = whole_call(lay, [rows, paired], [(64, 4096, bf16)], [keep_b])
     paired = lax.ppermute(rows, "x", ring_pair("x", False))
     a1, b1, b2, b3, keep_a, keep_b = whole_call(
         split_second,
         [keep_a, a1, a2, a3, keep_b, b1],
-        [(128, 640, i16)] * 4 + [(128, 512, f32)] * 2,
-    )
-    a1, b1, b2, b3 = send(a1, "zh", 1), send(b1, "y", 1), send(b2, "y", 2), send(b3, "y", 3)
+        [(528, 128, i16)] * 4 + [(128, 512, f32)] * 2,
+    )
+    b2, a1, b1, b3 = send(b2, "y", 2), send(a1, "zh", 1), send(b1, "y", 1), send(b3, "y", 3)
 
     (rows,) = whole_call(lay, [rows, paired], [(128, 4096, bf16)], [keep_a])
     gathered = jnp.concatenate([rows, shift(rows, "c", 1)], axis=0)
@@ -375,10 +410,8 @@
     head_grad = lax.dot_general(
         hidden_all, grad_logits, (((0,), (0,)), ((), ())), preferred_element_type=f32
     ).astype(bf16)
-    sorted_grad = lax.dot_general(
-        placing(token_order(me)), grad_logits, (((0,), (0,)), ((), ())), preferred_element_type=f32
-    ).astype(bf16)
-    hidden_grad = scatter_rows(*grad_rows(sorted_grad, student_head))
+    turn = (token_order(me)[:, None] == lax.broadcasted_iota(jnp.int32, (1, tokens), 1)).astype(bf16)
+    hidden_grad = scatter_rows(*grad_rows(grad_logits, turn, student_head), [head_grad])
     return (loss, head_grad, hidden_grad)
 
 

time: 144 us -> 134 us (0.931)
  Pallas kernels: 22.6 us -> 17.5 us
  waiting for transfers between devices: 56.4 us -> 52.1 us
  local copies, waits for them, and re-layouts: 4.46 us -> 7.12 us
  matrix products: 5.68 us -> 3.34 us
    ppermute x17, waiting for transfers between devices: 37.1 us -> 30.5 us  [send(): lax.ppermute(value, axis, [(i, (i + step) % size) for i in range(size)])]
    pallas_call x4, Pallas kernels: 21.5 us -> 16.2 us  [the longest x1 6.75 us: far_products(): pl.pallas_call(kernel, in_specs=[in_smem, anywhere, anywhere], out_specs=...]
    unnamed x21 -> x19, local copies, waits for them, and re-layouts: 4.03 us -> 6.68 us
    dot_general x1, matrix products: 3.31 us -> 1.3 us  [body(): lax.dot_general(hidden_all, grad_logits, (((0,), (0,)), ((), ())), prefer...]
  transfers between devices with their start and end apart: 36 -> 36, of which waited for: 18 -> 19; matrix products, arithmetic and copies ran while one was open for 4% -> 3% of each run, Pallas kernels for 12% -> 12%
where the time goes in v2:
time: 134 us
  waiting for transfers between devices  52.1 us (39%)
  starting transfers between devices  47.6 us (36%)
  Pallas kernels  17.5 us (13%)
  local copies, waits for them, and re-layouts  7.12 us (5%)
  other arithmetic  3.54 us (3%)
  matrix products  3.34 us (2%)
  between operations  2.89 us (2%)
    ppermute x17, waiting for transfers between devices, send(): lax.ppermute(value, axis, [(i, (i + step) % size) for i in range(size)])  30.5 us
    ppermute x17, starting transfers between devices, send(): lax.ppermute(value, axis, [(i, (i + step) % size) for i in range(size)])  18.8 us
    ppermute x9, starting transfers between devices, cross_z(): return lax.ppermute(value, ('zl', 'zh'), pairs)  15.5 us
    ppermute x4, waiting for transfers between devices, merge_all(): stats = merge(stats, lax.ppermute(stats, axis, ring_pair(axis, first)))  13.4 us
    pallas_call x1, Pallas kernels, far_products(): pl.pallas_call(kernel, in_specs=[in_smem, anywhere, anywhere], out_specs=...  6.75 us
    unnamed x19, local copies, waits for them, and re-layouts  6.68 us
    ppermute x9, waiting for transfers between devices, cross_z(): return lax.ppermute(value, ('zl', 'zh'), pairs)  6.09 us
    ppermute x4, starting transfers between devices, shift(): lax.ppermute(value, axis, [((i + step) % size, i) for i in range(size)])  4.95 us
  transfers between devices with their start and end apart: 36, of which 19 were waited for; matrix products, arithmetic and copies ran while one was open for 3% of the time, Pallas kernels for 12%

profile of v2, /device:TPU:0, one launch (start us, length us, event | category | flops | bytes accessed | tf_op | source)
XLA Modules:
  0.0 134.1 jit_solution(8611692571392502727)
XLA Ops:
  0.6 2.1 %collective-permute-start.1 = (bf16[2,4096]{1,0:T(2,128)(2,1)}, bf16[2,4096]{1,0:T(2,128)(2,1)S(1)}, u32[]{:S(2)}, u32[]{:S(2)}) collective-permute-start(bf16[2,4096]{1,0:T(2,128)(2,1)} %r0.1), channel_id=1, source_target_pairs={{0,64},{8,72},{64,0},{72,8},{1,65},{9,73},{65,1},{73,9},{2,66},{10... | collective-permute-start | bytes 49160 | tf_op jit(solution)/shard_map/ppermute | solution.py:27
  2.7 3.6 %collective-permute-start.2 = (bf16[2,4096]{1,0:T(2,128)(2,1)}, bf16[2,4096]{1,0:T(2,128)(2,1)S(1)}, u32[]{:S(2)}, u32[]{:S(2)}) collective-permute-start(bf16[2,4096]{1,0:T(2,128)(2,1)} %r0.1), channel_id=1, source_target_pairs={{0,8},{8,0},{64,72},{72,64},{1,9},{9,1},{65,73},{73,65},{2,10},{10... | collective-permute-start | bytes 49160 | tf_op jit(solution)/shard_map/ppermute | solution.py:27
  6.3 1.0 copy-done.1
  7.4 6.8 %shard_map.77 = s16[8,256,640]{2,1,0:T(8,128)(2,1)S(1)} custom-call(s32[8]{0:T(128)S(1)} %get-tuple-element.64.order_ref, bf16[256,1024]{1,0:T(8,128)(2,1)S(1)} %copy-done.1, bf16[1024,8192]{1,0:T(8,128)(2,1)} %head_ref.6), custom_call_target="tpu_custom_call" | custom-call | flops 6000000000 | bytes 15000000 | tf_op jit(solution)/shard_map/pallas_call | solution.py:145
  14.4 3.1 %collective-permute-start.4 = (bf16[8,4096]{1,0:T(8,128)(2,1)S(1)}, bf16[8,4096]{1,0:T(8,128)(2,1)S(1)}, u32[]{:S(2)}, u32[]{:S(2)}) collective-permute-start(bf16[8,4096]{1,0:T(8,128)(2,1)S(1)} %shard_map.78.refs_0_), channel_id=1, source_target_pairs={{2,0},{4,2},{6,4},{0,6},{3,1},{5,3},{7,5},{1,7},{10,8},{12,10},{14... | collective-permute-start | bytes 196616 | tf_op jit(solution)/shard_map/ppermute | solution.py:17
  17.5 0.6 collective-permute-start.5
  18.1 1.0 collective-permute-start.6
  19.1 3.6 %shard_map.76.first_ref = f32[4,256,512]{2,1,0:T(8,128)S(1)} custom-call(s32[4]{0:T(128)S(1)} %get-tuple-element.198.order_ref, bf16[256,1024]{1,0:T(8,128)(2,1)S(1)} %copy-done.2, bf16[1024,8192]{1,0:T(8,128)(2,1)} %head_ref.6), custom_call_target="tpu_custom_call" | custom-call | flops 4000000000 | bytes 10000000 | tf_op jit(solution)/shard_map/pallas_call | solution.py:170
  22.7 1.2 collective-permute-done.5.refs_2_
  23.9 0.7 collective-permute-done.6.refs_3_
  24.6 1.6 %collective-permute-start.15 = (bf16[32,4096]{1,0:T(8,128)(2,1)S(1)}, bf16[32,4096]{1,0:T(8,128)(2,1)S(1)}, u32[]{:S(2)}, u32[]{:S(2)}) collective-permute-start(bf16[32,4096]{1,0:T(8,128)(2,1)S(1)} %shard_map.79.refs_0_), channel_id=1, source_target_pairs={{0,16},{16,0},{32,48},{48,32},{1,17},{17,1},{33,49},{49,33},{2,18}... | collective-permute-start | bytes 786440 | tf_op jit(solution)/shard_map/ppermute | solution.py:354
  26.2 4.4 %shard_map.80 = (s16[1040,128]{1,0:T(8,128)(2,1)S(1)}, s16[1040,128]{1,0:T(8,128)(2,1)S(1)}, s16[1040,128]{1,0:T(8,128)(2,1)S(1)}, s16[2064,128]{1,0:T(8,128)(2,...) custom-call(s32[4]{0:T(128)S(1)} %get-tuple-element.199.order_ref, bf16[256,1024]{1,0:T(8,128)(2,1)S(1)} %copy-done.2, ...), custom_call_target="tpu_custom_call" | custom-call | flops 7000000000 | bytes 17500000 | tf_op jit(solution)/shard_map/pallas_call | solution.py:217
  30.6 1.9 %collective-permute-start.10 = (s16[2064,128]{1,0:T(8,128)(2,1)S(1)}, s16[2064,128]{1,0:T(8,128)(2,1)S(1)}, u32[]{:S(2)}, u32[]{:S(2)}) collective-permute-start(s16[2064,128]{1,0:T(8,128)(2,1)S(1)} %get-tuple-element.24), channel_id=1, source_target_pairs={{0,8},{8,0},{1,9},{9,1},{2,10},{10,2},{3,11},{11,3},{4,12},{12,4},... | collective-permute-start | bytes 1585160 | tf_op jit(solution)/shard_map/ppermute | solution.py:22
  32.6 0.2 collective-permute-done.15.refs_1_
  32.8 2.8 %collective-permute-start.16 = (bf16[64,4096]{1,0:T(8,128)(2,1)S(1)}, bf16[64,4096]{1,0:T(8,128)(2,1)S(1)}, u32[]{:S(2)}, u32[]{:S(2)}) collective-permute-start(bf16[64,4096]{1,0:T(8,128)(2,1)S(1)} %shard_map.82.refs_0_), channel_id=1, source_target_pairs={{0,48},{48,0},{16,32},{32,16},{1,49},{49,1},{17,33},{33,17},{2,50}... | collective-permute-start | bytes 1572872 | tf_op jit(solution)/shard_map/ppermute | solution.py:363
  35.7 1.6 %collective-permute-start.8 = (s16[1040,128]{1,0:T(8,128)(2,1)S(1)}, s16[1040,128]{1,0:T(8,128)(2,1)S(1)}, u32[]{:S(2)}, u32[]{:S(2)}) collective-permute-start(s16[1040,128]{1,0:T(8,128)(2,1)S(1)} %get-tuple-element.21), channel_id=1, source_target_pairs={{0,4},{2,6},{4,0},{6,2},{1,5},{3,7},{5,1},{7,3},{8,12},{10,14},{12... | collective-permute-start | bytes 798728 | tf_op jit(solution)/shard_map/ppermute | solution.py:22
  37.3 1.6 %collective-permute-start.9 = (s16[1040,128]{1,0:T(8,128)(2,1)S(1)}, s16[1040,128]{1,0:T(8,128)(2,1)S(1)}, u32[]{:S(2)}, u32[]{:S(2)}) collective-permute-start(s16[1040,128]{1,0:T(8,128)(2,1)S(1)} %get-tuple-element.22), channel_id=1, source_target_pairs={{0,6},{2,0},{4,2},{6,4},{1,7},{3,1},{5,3},{7,5},{8,14},{10,8},{12,... | collective-permute-start | bytes 798728 | tf_op jit(solution)/shard_map/ppermute | solution.py:22
  38.9 10.7 %collective-permute-done.7.r1 = s16[1040,128]{1,0:T(8,128)(2,1)S(1)} collective-permute-done((s16[1040,128]{1,0:T(8,128)(2,1)S(1)}, s16[1040,128]{1,0:T(8,128)(2,1)S(1)}, u32[]{:S(2)}, u32[]{:S(2)}) %collective-permute-start.7) | collective-permute-done | bytes 266272 | tf_op jit(solution)/shard_map/ppermute | solution.py:22
  49.7 0.6 collective-permute-done.9.r3
  50.3 0.9 shard_map.81
  51.2 0.3 collective-permute-start.17
  51.6 1.9 %collective-permute-start.11 = (s16[528,128]{1,0:T(8,128)(2,1)S(1)}, s16[528,128]{1,0:T(8,128)(2,1)S(1)}, u32[]{:S(2)}, u32[]{:S(2)}) collective-permute-start(s16[528,128]{1,0:T(8,128)(2,1)S(1)} %get-tuple-element.26), channel_id=1, source_target_pairs={{0,8},{8,0},{1,9},{9,1},{2,10},{10,2},{3,11},{11,3},{4,12},{12,4},... | collective-permute-start | bytes 405512 | tf_op jit(solution)/shard_map/ppermute | solution.py:22
  53.5 0.2 collective-permute-start.12
  53.8 3.6 %collective-permute-start.13 = (s16[528,128]{1,0:T(8,128)(2,1)S(1)}, s16[528,128]{1,0:T(8,128)(2,1)S(1)}, u32[]{:S(2)}, u32[]{:S(2)}) collective-permute-start(s16[528,128]{1,0:T(8,128)(2,1)S(1)} %get-tuple-element.29), channel_id=1, source_target_pairs={{0,4},{2,6},{4,0},{6,2},{1,5},{3,7},{5,1},{7,3},{8,12},{10,14},{12... | collective-permute-start | bytes 405512 | tf_op jit(solution)/shard_map/ppermute | solution.py:22
  57.3 0.7 convolution_convert_fusion.1
  58.1 1.4 %copy-done.3 = bf16[4096,512]{1,0:T(8,128)(2,1)S(1)} copy-done((bf16[4096,512]{1,0:T(8,128)(2,1)S(1)}, bf16[4096,512]{1,0:T(8,128)(2,1)}, u32[]{:S(2)}) %copy-start.3) | copy-done | bytes 4194328
  59.5 1.3 fusion.59
  60.9 3.0 %collective-permute-done.13.r2 = s16[528,128]{1,0:T(8,128)(2,1)S(1)} collective-permute-done((s16[528,128]{1,0:T(8,128)(2,1)S(1)}, s16[528,128]{1,0:T(8,128)(2,1)S(1)}, u32[]{:S(2)}, u32[]{:S(2)}) %collective-permute-start.13) | collective-permute-done | bytes 135200 | tf_op jit(solution)/shard_map/ppermute | solution.py:22
  63.9 0.3 shard_map.84
  64.4 0.5 multiply_reduce_fusion.1
  65.0 1.2 collective-permute-done.18
  66.2 0.3 collective-permute-start.19
  66.5 3.4 %collective-permute-done.19 = f32[8,256]{1,0:T(8,128)S(1)} collective-permute-done((f32[8,256]{1,0:T(8,128)S(1)}, f32[8,256]{1,0:T(8,128)S(1)}, u32[]{:S(2)}, u32[]{:S(2)}) %collective-permute-start.19) | collective-permute-done | bytes 8224 | tf_op jit(solution)/shard_map/ppermute | solution.py:57
  70.0 0.6 collective-permute-start.20
  70.6 4.4 %collective-permute-done.20 = f32[8,256]{1,0:T(8,128)S(1)} collective-permute-done((f32[8,256]{1,0:T(8,128)S(1)}, f32[8,256]{1,0:T(8,128)S(1)}, u32[]{:S(2)}, u32[]{:S(2)}) %collective-permute-start.20) | collective-permute-done | bytes 8224 | tf_op jit(solution)/shard_map/ppermute | solution.py:57
  75.1 0.4 collective-permute-start.21
  75.4 3.4 %collective-permute-done.21 = f32[8,256]{1,0:T(8,128)S(1)} collective-permute-done((f32[8,256]{1,0:T(8,128)S(1)}, f32[8,256]{1,0:T(8,128)S(1)}, u32[]{:S(2)}, u32[]{:S(2)}) %collective-permute-start.21) | collective-permute-done | bytes 8224 | tf_op jit(solution)/shard_map/ppermute | solution.py:57
  78.9 2.7 %collective-permute-start.22 = (f32[8,256]{1,0:T(8,128)S(1)}, f32[8,256]{1,0:T(8,128)S(1)}, u32[]{:S(2)}, u32[]{:S(2)}) collective-permute-start(f32[8,256]{1,0:T(8,128)S(1)} %stack.37), channel_id=1, source_target_pairs={{0,6},{6,0},{2,4},{4,2},{1,7},{7,1},{3,5},{5,3},{8,14},{14,8},{10,... | collective-permute-start | bytes 24584 | tf_op jit(solution)/shard_map/ppermute | solution.py:57
  81.6 2.2 %collective-permute-done.22 = f32[8,256]{1,0:T(8,128)S(1)} collective-permute-done((f32[8,256]{1,0:T(8,128)S(1)}, f32[8,256]{1,0:T(8,128)S(1)}, u32[]{:S(2)}, u32[]{:S(2)}) %collective-permute-start.22) | collective-permute-done | bytes 8224 | tf_op jit(solution)/shard_map/ppermute | solution.py:57
  83.9 2.3 %collective-permute-start.23 = (f32[8,256]{1,0:T(8,128)S(1)}, f32[8,256]{1,0:T(8,128)S(1)}, u32[]{:S(2)}, u32[]{:S(2)}) collective-permute-start(f32[8,256]{1,0:T(8,128)S(1)} %stack.38), channel_id=1, source_target_pairs={{0,64},{8,72},{64,0},{72,8},{1,65},{9,73},{65,1},{73,9},{2,66},{10... | collective-permute-start | bytes 24584 | tf_op jit(solution)/shard_map/ppermute | solution.py:27
  86.3 1.7 %collective-permute-start.24 = (f32[8,256]{1,0:T(8,128)S(1)}, f32[8,256]{1,0:T(8,128)S(1)}, u32[]{:S(2)}, u32[]{:S(2)}) collective-permute-start(f32[8,256]{1,0:T(8,128)S(1)} %stack.38), channel_id=1, source_target_pairs={{0,8},{8,0},{64,72},{72,64},{1,9},{9,1},{65,73},{73,65},{2,10},{10... | collective-permute-start | bytes 24584 | tf_op jit(solution)/shard_map/ppermute | solution.py:27
  88.0 1.0 collective-permute-start.25
  89.1 2.5 %collective-permute-done.24 = f32[8,256]{1,0:T(8,128)S(1)} collective-permute-done((f32[8,256]{1,0:T(8,128)S(1)}, f32[8,256]{1,0:T(8,128)S(1)}, u32[]{:S(2)}, u32[]{:S(2)}) %collective-permute-start.24) | collective-permute-done | bytes 8224 | tf_op jit(solution)/shard_map/ppermute | solution.py:27
  91.5 1.4 %collective-permute-done.25 = f32[8,256]{1,0:T(8,128)S(1)} collective-permute-done((f32[8,256]{1,0:T(8,128)S(1)}, f32[8,256]{1,0:T(8,128)S(1)}, u32[]{:S(2)}, u32[]{:S(2)}) %collective-permute-start.25) | collective-permute-done | bytes 8224 | tf_op jit(solution)/shard_map/ppermute | solution.py:27
  93.0 0.7 add_reduce_fusion
  93.6 0.3 fusion.5.grad_ref
  93.9 2.2 %copy-done.4 = bf16[4096,512]{1,0:T(8,128)(2,1)S(1)} copy-done((bf16[4096,512]{1,0:T(8,128)(2,1)S(1)}, bf16[4096,512]{1,0:T(8,128)(2,1)}, u32[]{:S(2)}) %copy-start.4) | copy-done | bytes 4194328
  96.1 1.4 %shard_map.85 = (f32[128,4096]{1,0:T(8,128)S(1)}, f32[128,4096]{1,0:T(8,128)S(1)}) custom-call(bf16[256,512]{1,0:T(8,128)(2,1)S(1)} %fusion.5.grad_ref, bf16[256,256]{1,0:T(8,128)(2,1)S(1)} %fusion.7.turn_ref, bf16[4096,512]{1,0:T(8,128)(2,1)S(1)} %copy-done.4), custom_call_target="tpu_custom_call" | custom-call | flops 3000000000 | bytes 7500000 | tf_op jit(solution)/shard_map/pallas_call | solution.py:318
  97.8 2.6 %collective-permute-done.26 = f16[128,4096]{1,0:T(8,128)(2,1)S(1)} collective-permute-done((f16[128,4096]{1,0:T(8,128)(2,1)S(1)}, f16[128,4096]{1,0:T(8,128)(2,1)S(1)}, u32[]{:S(2)}, u32[]{:S(2)}) %collective-permute-start.26) | collective-permute-done | bytes 1048608 | tf_op jit(solution)/shard_map/ppermute | solution.py:22
  100.4 0.5 multiply_convert_fusion
  101.2 2.0 %collective-permute-start.28 = (f16[32,4096]{1,0:T(8,128)(2,1)S(1)}, f16[32,4096]{1,0:T(8,128)(2,1)S(1)}, u32[]{:S(2)}, u32[]{:S(2)}) collective-permute-start(f16[32,4096]{1,0:T(8,128)(2,1)S(1)} %get-tuple-element.68), channel_id=1, source_target_pairs={{0,16},{16,32},{32,48},{48,0},{1,17},{17,33},{33,49},{49,1},{2,18}... | collective-permute-start | bytes 786440 | tf_op jit(solution)/shard_map/ppermute | solution.py:22
  103.1 1.3 collective-permute-start.29
  104.5 7.4 %collective-permute-done.27 = f16[32,4096]{1,0:T(8,128)(2,1)S(1)} collective-permute-done((f16[32,4096]{1,0:T(8,128)(2,1)S(1)}, f16[32,4096]{1,0:T(8,128)(2,1)S(1)}, u32[]{:S(2)}, u32[]{:S(2)}) %collective-permute-start.27) | collective-permute-done | bytes 262176 | tf_op jit(solution)/shard_map/ppermute | solution.py:22
  111.8 4.6 %collective-permute-done.28 = f16[32,4096]{1,0:T(8,128)(2,1)S(1)} collective-permute-done((f16[32,4096]{1,0:T(8,128)(2,1)S(1)}, f16[32,4096]{1,0:T(8,128)(2,1)S(1)}, u32[]{:S(2)}, u32[]{:S(2)}) %collective-permute-start.28) | collective-permute-done | bytes 262176 | tf_op jit(solution)/shard_map/ppermute | solution.py:22
  116.6 1.0 collective-permute-start.30
  117.6 2.6 %collective-permute-start.31 = (f16[8,4096]{1,0:T(8,128)(2,1)S(1)}, f16[8,4096]{1,0:T(8,128)(2,1)S(1)}, u32[]{:S(2)}, u32[]{:S(2)}) collective-permute-start(f16[8,4096]{1,0:T(8,128)(2,1)S(1)} %get-tuple-element.71), channel_id=1, source_target_pairs={{0,2},{2,4},{4,6},{6,0},{1,3},{3,5},{5,7},{7,1},{8,10},{10,12},{12... | collective-permute-start | bytes 196616 | tf_op jit(solution)/shard_map/ppermute | solution.py:22
  120.3 0.6 collective-permute-start.32
  120.9 1.3 convolution_convert_fusion.rest_0_
  122.2 2.0 %copy-done = bf16[4096,512]{1,0:T(8,128)(2,1)} copy-done((bf16[4096,512]{1,0:T(8,128)(2,1)}, bf16[4096,512]{1,0:T(8,128)(2,1)S(1)}, u32[]{:S(2)}) %copy-start) | copy-done | bytes 4194328
  124.2 0.3 collective-permute-done.32
  124.7 2.5 %collective-permute-start.34 = (f32[2,4096]{1,0:T(2,128)S(1)}, f32[2,4096]{1,0:T(2,128)S(1)}, u32[]{:S(2)}, u32[]{:S(2)}) collective-permute-start(f32[2,4096]{1,0:T(2,128)S(1)} %get-tuple-element.72), channel_id=1, source_target_pairs={{0,8},{8,0},{64,72},{72,64},{1,9},{9,1},{65,73},{73,65},{2,10},{10... | collective-permute-start | bytes 98312 | tf_op jit(solution)/shard_map/ppermute | solution.py:27
  127.2 2.2 %collective-permute-start.35 = (f32[2,4096]{1,0:T(2,128)S(1)}, f32[2,4096]{1,0:T(2,128)S(1)}, u32[]{:S(2)}, u32[]{:S(2)}) collective-permute-start(f32[2,4096]{1,0:T(2,128)S(1)} %get-tuple-element.73), channel_id=1, source_target_pairs={{0,72},{8,64},{64,8},{72,0},{1,73},{9,65},{65,9},{73,1},{2,74},{10... | collective-permute-start | bytes 98312 | tf_op jit(solution)/shard_map/ppermute | solution.py:27
  130.2 2.1 %collective-permute-done.35 = f32[2,4096]{1,0:T(2,128)S(1)} collective-permute-done((f32[2,4096]{1,0:T(2,128)S(1)}, f32[2,4096]{1,0:T(2,128)S(1)}, u32[]{:S(2)}, u32[]{:S(2)}) %collective-permute-start.35) | collective-permute-done | bytes 32800 | tf_op jit(solution)/shard_map/ppermute | solution.py:27
  132.3 0.6 slice_add_fusion.1
  (82 shorter events, 2.3 us)
Async XLA Ops:
  0.6 13.7 %collective-permute-start.1 = (bf16[2,4096]{1,0:T(2,128)(2,1)}, bf16[2,4096]{1,0:T(2,128)(2,1)S(1)}, u32[]{:S(2)}, u32[]{:S(2)}) collective-permute-start(bf16[2,4096]{1,0:T(2,128)(2,1)} %r0.1), channel_id=1, source_target_pairs={{0,64},{8,72},{64,0},{72,8},{1,65},{9,73},{65,1},{73,9},{2,66},{10... | collective-permute-start | bytes 49160 | tf_op jit(solution)/shard_map/ppermute | solution.py:27
  2.7 11.6 %collective-permute-start.2 = (bf16[2,4096]{1,0:T(2,128)(2,1)}, bf16[2,4096]{1,0:T(2,128)(2,1)S(1)}, u32[]{:S(2)}, u32[]{:S(2)}) collective-permute-start(bf16[2,4096]{1,0:T(2,128)(2,1)} %r0.1), channel_id=1, source_target_pairs={{0,8},{8,0},{64,72},{72,64},{1,9},{9,1},{65,73},{73,65},{2,10},{10... | collective-permute-start | bytes 49160 | tf_op jit(solution)/shard_map/ppermute | solution.py:27
  6.3 8.0 %collective-permute-start.3 = (bf16[2,4096]{1,0:T(2,128)(2,1)}, bf16[2,4096]{1,0:T(2,128)(2,1)S(1)}, u32[]{:S(2)}, u32[]{:S(2)}) collective-permute-start(bf16[2,4096]{1,0:T(2,128)(2,1)} %r0.1), channel_id=1, source_target_pairs={{0,72},{8,64},{64,8},{72,0},{1,73},{9,65},{65,9},{73,1},{2,74},{10... | collective-permute-start | bytes 49160 | tf_op jit(solution)/shard_map/ppermute | solution.py:27
  6.3 1.0 copy-start.1
  7.4 7.0 %copy-start.5 = (bf16[2,4096]{1,0:T(2,128)(2,1)S(1)}, bf16[2,4096]{1,0:T(2,128)(2,1)}, u32[]{:S(2)}) copy-start(bf16[2,4096]{1,0:T(2,128)(2,1)} %r0.1) | copy-start | bytes 49156
  14.1 4.9 %copy-start.2 = (bf16[256,1024]{1,0:T(8,128)(2,1)S(1)}, bf16[256,1024]{1,0:T(8,128)(2,1)}, u32[]{:S(2)}) copy-start(bf16[256,1024]{1,0:T(8,128)(2,1)} %hidden_ref.5) | copy-start | bytes 1572868
  14.1 12.0 %collective-permute-start = (s16[8,256,640]{2,1,0:T(8,128)(2,1)S(1)}, s16[8,256,640]{2,1,0:T(8,128)(2,1)S(1)}, u32[]{:S(2)}, u32[]{:S(2)}) collective-permute-start(s16[8,256,640]{2,1,0:T(8,128)(2,1)S(1)} %shard_map.77), channel_id=1, source_target_pairs={{0,1},{1,0},{2,3},{3,2},{4,5},{5,4},{6,7},{7,6},{8,9},{9,8},{10,11... | collective-permute-start | bytes 7864328 | tf_op jit(solution)/shard_map/ppermute | solution.py:22
  14.4 8.3 %collective-permute-start.4 = (bf16[8,4096]{1,0:T(8,128)(2,1)S(1)}, bf16[8,4096]{1,0:T(8,128)(2,1)S(1)}, u32[]{:S(2)}, u32[]{:S(2)}) collective-permute-start(bf16[8,4096]{1,0:T(8,128)(2,1)S(1)} %shard_map.78.refs_0_), channel_id=1, source_target_pairs={{2,0},{4,2},{6,4},{0,6},{3,1},{5,3},{7,5},{1,7},{10,8},{12,10},{14... | collective-permute-start | bytes 196616 | tf_op jit(solution)/shard_map/ppermute | solution.py:17
  17.5 6.4 %collective-permute-start.5 = (bf16[8,4096]{1,0:T(8,128)(2,1)S(1)}, bf16[8,4096]{1,0:T(8,128)(2,1)S(1)}, u32[]{:S(2)}, u32[]{:S(2)}) collective-permute-start(bf16[8,4096]{1,0:T(8,128)(2,1)S(1)} %shard_map.78.refs_0_), channel_id=1, source_target_pairs={{4,0},{6,2},{0,4},{2,6},{5,1},{7,3},{1,5},{3,7},{12,8},{14,10},{8,... | collective-permute-start | bytes 196616 | tf_op jit(solution)/shard_map/ppermute | solution.py:17
  18.1 6.5 %collective-permute-start.6 = (bf16[8,4096]{1,0:T(8,128)(2,1)S(1)}, bf16[8,4096]{1,0:T(8,128)(2,1)S(1)}, u32[]{:S(2)}, u32[]{:S(2)}) collective-permute-start(bf16[8,4096]{1,0:T(8,128)(2,1)S(1)} %shard_map.78.refs_0_), channel_id=1, source_target_pairs={{6,0},{0,2},{2,4},{4,6},{7,1},{1,3},{3,5},{5,7},{14,8},{8,10},{10,... | collective-permute-start | bytes 196616 | tf_op jit(solution)/shard_map/ppermute | solution.py:17
  24.6 8.2 %collective-permute-start.15 = (bf16[32,4096]{1,0:T(8,128)(2,1)S(1)}, bf16[32,4096]{1,0:T(8,128)(2,1)S(1)}, u32[]{:S(2)}, u32[]{:S(2)}) collective-permute-start(bf16[32,4096]{1,0:T(8,128)(2,1)S(1)} %shard_map.79.refs_0_), channel_id=1, source_target_pairs={{0,16},{16,0},{32,48},{48,32},{1,17},{17,1},{33,49},{49,33},{2,18}... | collective-permute-start | bytes 786440 | tf_op jit(solution)/shard_map/ppermute | solution.py:354
  30.6 19.7 %collective-permute-start.10 = (s16[2064,128]{1,0:T(8,128)(2,1)S(1)}, s16[2064,128]{1,0:T(8,128)(2,1)S(1)}, u32[]{:S(2)}, u32[]{:S(2)}) collective-permute-start(s16[2064,128]{1,0:T(8,128)(2,1)S(1)} %get-tuple-element.24), channel_id=1, source_target_pairs={{0,8},{8,0},{1,9},{9,1},{2,10},{10,2},{3,11},{11,3},{4,12},{12,4},... | collective-permute-start | bytes 1585160 | tf_op jit(solution)/shard_map/ppermute | solution.py:22
  32.8 18.3 %collective-permute-start.16 = (bf16[64,4096]{1,0:T(8,128)(2,1)S(1)}, bf16[64,4096]{1,0:T(8,128)(2,1)S(1)}, u32[]{:S(2)}, u32[]{:S(2)}) collective-permute-start(bf16[64,4096]{1,0:T(8,128)(2,1)S(1)} %shard_map.82.refs_0_), channel_id=1, source_target_pairs={{0,48},{48,0},{16,32},{32,16},{1,49},{49,1},{17,33},{33,17},{2,50}... | collective-permute-start | bytes 1572872 | tf_op jit(solution)/shard_map/ppermute | solution.py:363
  35.7 14.0 %collective-permute-start.7 = (s16[1040,128]{1,0:T(8,128)(2,1)S(1)}, s16[1040,128]{1,0:T(8,128)(2,1)S(1)}, u32[]{:S(2)}, u32[]{:S(2)}) collective-permute-start(s16[1040,128]{1,0:T(8,128)(2,1)S(1)} %get-tuple-element.20), channel_id=1, source_target_pairs={{0,2},{2,4},{4,6},{6,0},{1,3},{3,5},{5,7},{7,1},{8,10},{10,12},{12... | collective-permute-start | bytes 798728 | tf_op jit(solution)/shard_map/ppermute | solution.py:22
  35.7 14.0 %collective-permute-start.8 = (s16[1040,128]{1,0:T(8,128)(2,1)S(1)}, s16[1040,128]{1,0:T(8,128)(2,1)S(1)}, u32[]{:S(2)}, u32[]{:S(2)}) collective-permute-start(s16[1040,128]{1,0:T(8,128)(2,1)S(1)} %get-tuple-element.21), channel_id=1, source_target_pairs={{0,4},{2,6},{4,0},{6,2},{1,5},{3,7},{5,1},{7,3},{8,12},{10,14},{12... | collective-permute-start | bytes 798728 | tf_op jit(solution)/shard_map/ppermute | solution.py:22
  37.3 13.0 %collective-permute-start.9 = (s16[1040,128]{1,0:T(8,128)(2,1)S(1)}, s16[1040,128]{1,0:T(8,128)(2,1)S(1)}, u32[]{:S(2)}, u32[]{:S(2)}) collective-permute-start(s16[1040,128]{1,0:T(8,128)(2,1)S(1)} %get-tuple-element.22), channel_id=1, source_target_pairs={{0,6},{2,0},{4,2},{6,4},{1,7},{3,1},{5,3},{7,5},{8,14},{10,8},{12,... | collective-permute-start | bytes 798728 | tf_op jit(solution)/shard_map/ppermute | solution.py:22
  51.2 6.1 %collective-permute-start.17 = (bf16[128,4096]{1,0:T(8,128)(2,1)S(1)}, bf16[128,4096]{1,0:T(8,128)(2,1)S(1)}, u32[]{:S(2)}, u32[]{:S(2)}) collective-permute-start(bf16[128,4096]{1,0:T(8,128)(2,1)S(1)} %shard_map.83), channel_id=1, source_target_pairs={{1,0},{0,1},{3,2},{2,3},{5,4},{4,5},{7,6},{6,7},{9,8},{8,9},{11,10... | collective-permute-start | bytes 3145736 | tf_op jit(solution)/shard_map/ppermute | solution.py:17
  51.6 9.3 %collective-permute-start.11 = (s16[528,128]{1,0:T(8,128)(2,1)S(1)}, s16[528,128]{1,0:T(8,128)(2,1)S(1)}, u32[]{:S(2)}, u32[]{:S(2)}) collective-permute-start(s16[528,128]{1,0:T(8,128)(2,1)S(1)} %get-tuple-element.26), channel_id=1, source_target_pairs={{0,8},{8,0},{1,9},{9,1},{2,10},{10,2},{3,11},{11,3},{4,12},{12,4},... | collective-permute-start | bytes 405512 | tf_op jit(solution)/shard_map/ppermute | solution.py:22
  53.5 7.3 %collective-permute-start.12 = (s16[528,128]{1,0:T(8,128)(2,1)S(1)}, s16[528,128]{1,0:T(8,128)(2,1)S(1)}, u32[]{:S(2)}, u32[]{:S(2)}) collective-permute-start(s16[528,128]{1,0:T(8,128)(2,1)S(1)} %get-tuple-element.28), channel_id=1, source_target_pairs={{0,2},{2,4},{4,6},{6,0},{1,3},{3,5},{5,7},{7,1},{8,10},{10,12},{12... | collective-permute-start | bytes 405512 | tf_op jit(solution)/shard_map/ppermute | solution.py:22
  53.8 10.1 %collective-permute-start.13 = (s16[528,128]{1,0:T(8,128)(2,1)S(1)}, s16[528,128]{1,0:T(8,128)(2,1)S(1)}, u32[]{:S(2)}, u32[]{:S(2)}) collective-permute-start(s16[528,128]{1,0:T(8,128)(2,1)S(1)} %get-tuple-element.29), channel_id=1, source_target_pairs={{0,4},{2,6},{4,0},{6,2},{1,5},{3,7},{5,1},{7,3},{8,12},{10,14},{12... | collective-permute-start | bytes 405512 | tf_op jit(solution)/shard_map/ppermute | solution.py:22
  57.3 2.2 %copy-start.3 = (bf16[4096,512]{1,0:T(8,128)(2,1)S(1)}, bf16[4096,512]{1,0:T(8,128)(2,1)}, u32[]{:S(2)}) copy-start(bf16[4096,512]{1,0:T(8,128)(2,1)} %head_ref.7) | copy-start | bytes 12582916
  57.3 6.6 %collective-permute-start.14 = (s16[528,128]{1,0:T(8,128)(2,1)S(1)}, s16[528,128]{1,0:T(8,128)(2,1)S(1)}, u32[]{:S(2)}, u32[]{:S(2)}) collective-permute-start(s16[528,128]{1,0:T(8,128)(2,1)S(1)} %get-tuple-element.30), channel_id=1, source_target_pairs={{0,6},{2,0},{4,2},{6,4},{1,7},{3,1},{5,3},{7,5},{8,14},{10,8},{12,... | collective-permute-start | bytes 405512 | tf_op jit(solution)/shard_map/ppermute | solution.py:22
  59.5 1.3 copy-start.6
  60.9 3.5 %copy-start.8 = (s32[256]{0:T(256)S(1)}, s32[256]{0:T(256)}, u32[]{:S(2)}) copy-start(s32[256]{0:T(256)} %param.9) | copy-start | bytes 3076
  64.9 1.2 collective-permute-start.18
  66.2 3.7 %collective-permute-start.19 = (f32[8,256]{1,0:T(8,128)S(1)}, f32[8,256]{1,0:T(8,128)S(1)}, u32[]{:S(2)}, u32[]{:S(2)}) collective-permute-start(f32[8,256]{1,0:T(8,128)S(1)} %stack.34), channel_id=1, source_target_pairs={{0,16},{16,0},{32,48},{48,32},{1,17},{17,1},{33,49},{49,33},{2,18}... | collective-permute-start | bytes 24584 | tf_op jit(solution)/shard_map/ppermute | solution.py:57
  70.0 4.9 %collective-permute-start.20 = (f32[8,256]{1,0:T(8,128)S(1)}, f32[8,256]{1,0:T(8,128)S(1)}, u32[]{:S(2)}, u32[]{:S(2)}) collective-permute-start(f32[8,256]{1,0:T(8,128)S(1)} %stack.35), channel_id=1, source_target_pairs={{0,48},{48,0},{16,32},{32,16},{1,49},{49,1},{17,33},{33,17},{2,50}... | collective-permute-start | bytes 24584 | tf_op jit(solution)/shard_map/ppermute | solution.py:57
  75.1 3.7 %collective-permute-start.21 = (f32[8,256]{1,0:T(8,128)S(1)}, f32[8,256]{1,0:T(8,128)S(1)}, u32[]{:S(2)}, u32[]{:S(2)}) collective-permute-start(f32[8,256]{1,0:T(8,128)S(1)} %stack.36), channel_id=1, source_target_pairs={{0,2},{2,0},{4,6},{6,4},{1,3},{3,1},{5,7},{7,5},{8,10},{10,8},{12,... | collective-permute-start | bytes 24584 | tf_op jit(solution)/shard_map/ppermute | solution.py:57
  78.9 4.9 %collective-permute-start.22 = (f32[8,256]{1,0:T(8,128)S(1)}, f32[8,256]{1,0:T(8,128)S(1)}, u32[]{:S(2)}, u32[]{:S(2)}) collective-permute-start(f32[8,256]{1,0:T(8,128)S(1)} %stack.37), channel_id=1, source_target_pairs={{0,6},{6,0},{2,4},{4,2},{1,7},{7,1},{3,5},{5,3},{8,14},{14,8},{10,... | collective-permute-start | bytes 24584 | tf_op jit(solution)/shard_map/ppermute | solution.py:57
  83.9 5.2 %collective-permute-start.23 = (f32[8,256]{1,0:T(8,128)S(1)}, f32[8,256]{1,0:T(8,128)S(1)}, u32[]{:S(2)}, u32[]{:S(2)}) collective-permute-start(f32[8,256]{1,0:T(8,128)S(1)} %stack.38), channel_id=1, source_target_pairs={{0,64},{8,72},{64,0},{72,8},{1,65},{9,73},{65,1},{73,9},{2,66},{10... | collective-permute-start | bytes 24584 | tf_op jit(solution)/shard_map/ppermute | solution.py:27
  86.3 5.2 %collective-permute-start.24 = (f32[8,256]{1,0:T(8,128)S(1)}, f32[8,256]{1,0:T(8,128)S(1)}, u32[]{:S(2)}, u32[]{:S(2)}) collective-permute-start(f32[8,256]{1,0:T(8,128)S(1)} %stack.38), channel_id=1, source_target_pairs={{0,8},{8,0},{64,72},{72,64},{1,9},{9,1},{65,73},{73,65},{2,10},{10... | collective-permute-start | bytes 24584 | tf_op jit(solution)/shard_map/ppermute | solution.py:27
  88.0 4.9 %collective-permute-start.25 = (f32[8,256]{1,0:T(8,128)S(1)}, f32[8,256]{1,0:T(8,128)S(1)}, u32[]{:S(2)}, u32[]{:S(2)}) collective-permute-start(f32[8,256]{1,0:T(8,128)S(1)} %stack.38), channel_id=1, source_target_pairs={{0,72},{8,64},{64,8},{72,0},{1,73},{9,65},{65,9},{73,1},{2,74},{10... | collective-permute-start | bytes 24584 | tf_op jit(solution)/shard_map/ppermute | solution.py:27
  93.9 2.2 %copy-start.4 = (bf16[4096,512]{1,0:T(8,128)(2,1)S(1)}, bf16[4096,512]{1,0:T(8,128)(2,1)}, u32[]{:S(2)}) copy-start(bf16[4096,512]{1,0:T(8,128)(2,1)} %head_ref.7) | copy-start | bytes 12582916
  97.7 2.7 %collective-permute-start.26 = (f16[128,4096]{1,0:T(8,128)(2,1)S(1)}, f16[128,4096]{1,0:T(8,128)(2,1)S(1)}, u32[]{:S(2)}, u32[]{:S(2)}) collective-permute-start(f16[128,4096]{1,0:T(8,128)(2,1)S(1)} %multiply_convert_fusion.1), channel_id=1, source_target_pairs={{0,1},{1,0},{2,3},{3,2},{4,5},{5,4},{6,7},{7,6},{8,9},{9,8},{10,11... | collective-permute-start | bytes 3145736 | tf_op jit(solution)/shard_map/ppermute | solution.py:22
  100.9 20.0 %copy-start.7 = (bf16[256,4096]{1,0:T(8,128)(2,1)S(1)}, bf16[256,4096]{1,0:T(8,128)(2,1)}, u32[]{:S(2)}) copy-start(bf16[256,4096]{1,0:T(8,128)(2,1)} %copy-done.6) | copy-start | bytes 6291460
  101.1 10.8 %collective-permute-start.27 = (f16[32,4096]{1,0:T(8,128)(2,1)S(1)}, f16[32,4096]{1,0:T(8,128)(2,1)S(1)}, u32[]{:S(2)}, u32[]{:S(2)}) collective-permute-start(f16[32,4096]{1,0:T(8,128)(2,1)S(1)} %get-tuple-element.66), channel_id=1, source_target_pairs={{0,32},{16,48},{32,0},{48,16},{1,33},{17,49},{33,1},{49,17},{2,34}... | collective-permute-start | bytes 786440 | tf_op jit(solution)/shard_map/ppermute | solution.py:22
  101.2 15.2 %collective-permute-start.28 = (f16[32,4096]{1,0:T(8,128)(2,1)S(1)}, f16[32,4096]{1,0:T(8,128)(2,1)S(1)}, u32[]{:S(2)}, u32[]{:S(2)}) collective-permute-start(f16[32,4096]{1,0:T(8,128)(2,1)S(1)} %get-tuple-element.68), channel_id=1, source_target_pairs={{0,16},{16,32},{32,48},{48,0},{1,17},{17,33},{33,49},{49,1},{2,18}... | collective-permute-start | bytes 786440 | tf_op jit(solution)/shard_map/ppermute | solution.py:22
  103.1 13.3 %collective-permute-start.29 = (f16[32,4096]{1,0:T(8,128)(2,1)S(1)}, f16[32,4096]{1,0:T(8,128)(2,1)S(1)}, u32[]{:S(2)}, u32[]{:S(2)}) collective-permute-start(f16[32,4096]{1,0:T(8,128)(2,1)S(1)} %get-tuple-element.67), channel_id=1, source_target_pairs={{0,48},{16,0},{32,16},{48,32},{1,49},{17,1},{33,17},{49,33},{2,50}... | collective-permute-start | bytes 786440 | tf_op jit(solution)/shard_map/ppermute | solution.py:22
  116.6 7.5 %collective-permute-start.30 = (f16[8,4096]{1,0:T(8,128)(2,1)S(1)}, f16[8,4096]{1,0:T(8,128)(2,1)S(1)}, u32[]{:S(2)}, u32[]{:S(2)}) collective-permute-start(f16[8,4096]{1,0:T(8,128)(2,1)S(1)} %get-tuple-element.69), channel_id=1, source_target_pairs={{0,4},{2,6},{4,0},{6,2},{1,5},{3,7},{5,1},{7,3},{8,12},{10,14},{12... | collective-permute-start | bytes 196616 | tf_op jit(solution)/shard_map/ppermute | solution.py:22
  117.6 6.6 %collective-permute-start.31 = (f16[8,4096]{1,0:T(8,128)(2,1)S(1)}, f16[8,4096]{1,0:T(8,128)(2,1)S(1)}, u32[]{:S(2)}, u32[]{:S(2)}) collective-permute-start(f16[8,4096]{1,0:T(8,128)(2,1)S(1)} %get-tuple-element.71), channel_id=1, source_target_pairs={{0,2},{2,4},{4,6},{6,0},{1,3},{3,5},{5,7},{7,1},{8,10},{10,12},{12... | collective-permute-start | bytes 196616 | tf_op jit(solution)/shard_map/ppermute | solution.py:22
  120.3 4.3 %collective-permute-start.32 = (f16[8,4096]{1,0:T(8,128)(2,1)S(1)}, f16[8,4096]{1,0:T(8,128)(2,1)S(1)}, u32[]{:S(2)}, u32[]{:S(2)}) collective-permute-start(f16[8,4096]{1,0:T(8,128)(2,1)S(1)} %get-tuple-element.70), channel_id=1, source_target_pairs={{0,6},{2,0},{4,2},{6,4},{1,7},{3,1},{5,3},{7,5},{8,14},{10,8},{12,... | collective-permute-start | bytes 196616 | tf_op jit(solution)/shard_map/ppermute | solution.py:22
  122.2 2.0 %copy-start = (bf16[4096,512]{1,0:T(8,128)(2,1)}, bf16[4096,512]{1,0:T(8,128)(2,1)S(1)}, u32[]{:S(2)}) copy-start(bf16[4096,512]{1,0:T(8,128)(2,1)S(1)} %convolution_convert_fusion.rest_0_) | copy-start | bytes 12582916
  124.6 5.4 %collective-permute-start.33 = (f32[2,4096]{1,0:T(2,128)S(1)}, f32[2,4096]{1,0:T(2,128)S(1)}, u32[]{:S(2)}, u32[]{:S(2)}) collective-permute-start(f32[2,4096]{1,0:T(2,128)S(1)} %get-tuple-element.74), channel_id=1, source_target_pairs={{0,64},{8,72},{64,0},{72,8},{1,65},{9,73},{65,1},{73,9},{2,66},{10... | collective-permute-start | bytes 98312 | tf_op jit(solution)/shard_map/ppermute | solution.py:27
  124.7 5.5 %collective-permute-start.34 = (f32[2,4096]{1,0:T(2,128)S(1)}, f32[2,4096]{1,0:T(2,128)S(1)}, u32[]{:S(2)}, u32[]{:S(2)}) collective-permute-start(f32[2,4096]{1,0:T(2,128)S(1)} %get-tuple-element.72), channel_id=1, source_target_pairs={{0,8},{8,0},{64,72},{72,64},{1,9},{9,1},{65,73},{73,65},{2,10},{10... | collective-permute-start | bytes 98312 | tf_op jit(solution)/shard_map/ppermute | solution.py:27
  127.2 5.1 %collective-permute-start.35 = (f32[2,4096]{1,0:T(2,128)S(1)}, f32[2,4096]{1,0:T(2,128)S(1)}, u32[]{:S(2)}, u32[]{:S(2)}) collective-permute-start(f32[2,4096]{1,0:T(2,128)S(1)} %get-tuple-element.73), channel_id=1, source_target_pairs={{0,72},{8,64},{64,8},{72,0},{1,73},{9,65},{65,9},{73,1},{2,74},{10... | collective-permute-start | bytes 98312 | tf_op jit(solution)/shard_map/ppermute | solution.py:27
